TPU v7x, 768 devices: a whole 4x8x12 slice. The times are simulated.
768 devices in a mesh: gx: 96 (over y, z), gy: 8 (over x, core).
Axes of the slice: x: 4, y: 8, z: 12, core: 2. Of those that a mesh axis runs over, the one named last changes fastest.
Arguments:
- disp: bfloat16 [49152, 4096], P(('gx', 'gy')), may hold values from -6 to 6
- adjoint: bfloat16 [49152, 4096], P(('gx', 'gy')), may hold values from -6 to 6
- tiles: bfloat16 [73728, 4096], P(('gx', 'gy')), may hold values from -0.75 to 0.75
- tile_rows: int32 [73728], P(('gx', 'gy')), may hold values from 0 to 63
- tile_cols: int32 [73728], P(('gx', 'gy')), may hold values from 0 to 95
- density: float32 [73728], P(('gx', 'gy')), may hold values from 0.1 to 1
- filter_weight: float32 [73728], P(('gx', 'gy')), may hold values from 0.2 to 2
- owner: int32 [73728, 1], P(('gx', 'gy')), may hold values from 0 to 7; in each aligned block of 96 rows (0 to 95, 96 to 191, ...) at most 96 rows name the same one
- region: int32 [73728], P(('gx', 'gy')), may hold values from 0 to 31
- face_x: int32 [768, 2, 12], P(('gx', 'gy')), may hold values from 0 to 63
- face_y: int32 [768, 2, 4], P(('gx', 'gy')), may hold values from 0 to 63
Outputs:
- filtered: float32 [24576, 128], P(('gx', 'gy'))
- compliance: float32 [64], replicated
Inputs may be any that keep to these rules, and one draw needn't show every extreme that they name: Among the 96 elements of one subdomain at most 96 name the same owner, a bound that some block reaches.
All inputs are finite; a program needn't handle non-finite values.
Results may differ from a plain program's by a relative error of at most 0.0005.
Values may be sent and summed in bfloat16 or wider, within the bound.
No kernel may reach another device: no remote copies, remote signals or barrier semaphores. Data moves between devices by JAX's collectives and lax.ppermute only.
A program may use at most 64 MiB of HBM per device.

v0:
```python
import math

import jax
import jax.numpy as jnp
from jax import lax
from jax.sharding import PartitionSpec as P

BS = 64
R = 64
NREG = 32
CAP = 96


def shifted(x, axis, by):
    size = lax.axis_size(axis)
    pairs = [(i, i + by) for i in range(size) if 0 <= i + by < size]
    return lax.ppermute(x, axis, pairs)


def across_columns(first, second, by):
    return shifted((first, second), "gx", by)


def across_rows(first, second, by):
    return shifted((first, second), "gy", by)


def shards(
    disp,
    adjoint,
    tiles,
    tile_rows,
    tile_cols,
    density,
    filter_weight,
    owner,
    region,
    face_x,
    face_y,
):
    lists_x = face_x[0]
    lists_y = face_y[0]
    low_x = across_columns(disp[lists_x[0]], adjoint[lists_x[0]], 1)
    high_x = across_columns(disp[lists_x[1]], adjoint[lists_x[1]], -1)
    low_y = across_rows(disp[lists_y[0]], adjoint[lists_y[0]], 1)
    high_y = across_rows(disp[lists_y[1]], adjoint[lists_y[1]], -1)
    disp_ext = jnp.concatenate([disp, low_x[0], high_x[0], low_y[0], high_y[0]], axis=0)
    adj_ext = jnp.concatenate([adjoint, low_x[1], high_x[1], low_y[1], high_y[1]], axis=0)
    count = tiles.shape[0]
    kmat = tiles.reshape(count, BS, BS)
    ucol = disp_ext[tile_cols].reshape(count, BS, R)
    lcol = adj_ext[tile_cols].reshape(count, BS, R)
    ku = jnp.einsum("tjk,tkr->tjr", kmat, ucol, preferred_element_type=jnp.float32)
    kl = jnp.einsum("tjk,tkr->tjr", kmat, lcol, preferred_element_type=jnp.float32)
    urow = disp[tile_rows].reshape(count, BS, R).astype(jnp.float32)
    lrow = adjoint[tile_rows].reshape(count, BS, R).astype(jnp.float32)
    cross = jnp.sum(lrow * ku + urow * kl, axis=1)
    energy = jnp.sum(urow * ku, axis=1) / math.sqrt(BS)
    sens = -(3.0 * density * density / (2.0 * math.sqrt(BS)))[:, None] * cross
    payload = filter_weight[:, None] * jnp.concatenate([sens, energy], axis=1)
    rows_y = lax.axis_size("gy")
    total_tiles = count * lax.axis_size("gx") * rows_y
    compliance = lax.psum(jnp.sum(energy, axis=0), ("gx", "gy")) / math.sqrt(total_tiles)
    target = owner[:, 0]
    onehot = (target[:, None] == jnp.arange(rows_y, dtype=jnp.int32)[None, :]).astype(jnp.int32)
    before = jnp.cumsum(onehot, axis=0) - onehot
    slot = jnp.sum(before * onehot, axis=1)
    position = target * CAP + slot
    buffer = jnp.zeros((rows_y * CAP, 2 * R), jnp.float32).at[position].set(payload)
    weights = jnp.zeros((rows_y * CAP,), jnp.float32).at[position].set(filter_weight)
    labels = jnp.full((rows_y * CAP,), NREG, jnp.int32).at[position].set(region)
    got_rows, got_weights = (
        lax.all_to_all(
            buffer.reshape(rows_y, CAP, 2 * R), "gy", split_axis=0, concat_axis=0, tiled=True
        ),
        lax.all_to_all(weights.reshape(rows_y, CAP), "gy", split_axis=0, concat_axis=0, tiled=True),
    )
    got_labels = lax.all_to_all(
        labels.reshape(rows_y, CAP), "gy", split_axis=0, concat_axis=0, tiled=True
    )
    flat_labels = got_labels.reshape(-1)
    sums = jax.ops.segment_sum(got_rows.reshape(-1, 2 * R), flat_labels, NREG + 1)[:NREG]
    totals = jax.ops.segment_sum(got_weights.reshape(-1), flat_labels, NREG + 1)[:NREG]
    filtered = sums / jnp.maximum(totals, 1.0)[:, None]
    return (filtered, compliance)


def solution(mesh):
    placed = (
        P(("gx", "gy"), None),
        P(("gx", "gy"), None),
        P(("gx", "gy"), None),
        P(("gx", "gy")),
        P(("gx", "gy")),
        P(("gx", "gy")),
        P(("gx", "gy")),
        P(("gx", "gy"), None),
        P(("gx", "gy")),
        P(("gx", "gy"), None, None),
        P(("gx", "gy"), None, None),
    )
    return jax.shard_map(
        shards, mesh=mesh, in_specs=placed, out_specs=(P(("gx", "gy"), None), P()), check_vma=False
    )
```

profile of v0, /device:TPU:1, one launch (start us, length us, event | category | flops | bytes accessed | tf_op | source)
XLA Modules:
  0.0 236.6 jit_solution(13731439817377765431)
XLA Ops:
  0.7 0.8 fusion.7
  1.6 0.8 select_reduce_fusion
  2.5 0.7 fusion.17
  3.2 1.0 scatter_custom_fusion
  4.2 0.7 all_to_all.15
  4.9 13.7 %all-to-all-start = ((s32[8,1,96]{2,1,0:T(1,128)}), s32[8,1,96]{2,1,0:T(1,128)S(1)}, u32[]{:S(2)}, u32[]{:S(2)}) async-start(s32[8,1,96]{2,1,0:T(1,128)} %all_to_all.15), calls=%async_computation | async-start | bytes 8192 | tf_op jit(solution)/shard_map/all_to_all | solution.py:78
  18.6 0.8 fusion.19
  19.4 1.8 gather_fusion.1
  21.2 1.3 collective-permute-start
  22.5 1.2 gather_fusion.2
  23.8 1.3 collective-permute-start.1
  25.7 3.5 %collective-permute-start.2 = (bf16[4,4096]{1,0:T(4,128)(2,1)S(1)}, bf16[4,4096]{1,0:T(4,128)(2,1)S(1)}, u32[]{:S(2)}, u32[]{:S(2)}) collective-permute-start(bf16[4,4096]{1,0:T(4,128)(2,1)S(1)} %gather_fusion.3), channel_id=1, source_target_pairs={{0,1},{1,2},{2,3},{3,4},{4,5},{5,6},{6,7},{8,9},{9,10},{10,11},{11... | collective-permute-start | bytes 98312 | tf_op jit(solution)/shard_map/ppermute | solution.py:17
  29.8 1.9 collective-permute-start.3
  31.8 1.3 gather_fusion.7
  33.0 4.3 %collective-permute-start.4 = (bf16[12,4096]{1,0:T(8,128)(2,1)}, bf16[12,4096]{1,0:T(8,128)(2,1)S(1)}, u32[]{:S(2)}, u32[]{:S(2)}) collective-permute-start(bf16[12,4096]{1,0:T(8,128)(2,1)} %gather_fusion.7), channel_id=1, source_target_pairs={{0,8},{8,16},{16,24},{24,32},{32,40},{40,48},{48,56},{56,64},{64,7... | collective-permute-start | bytes 294920 | tf_op jit(solution)/shard_map/ppermute | solution.py:17
  37.9 1.3 gather_fusion.8
  39.2 1.2 gather_fusion.9
  40.4 1.2 gather_fusion.10
  41.6 1.0 scatter_custom_fusion.3
  42.6 0.7 all_to_all.18
  43.3 1.3 collective-permute-start.5
  44.6 3.9 %collective-permute-start.6 = (bf16[4,4096]{1,0:T(4,128)(2,1)}, bf16[4,4096]{1,0:T(4,128)(2,1)}, u32[]{:S(2)}, u32[]{:S(2)}) collective-permute-start(bf16[4,4096]{1,0:T(4,128)(2,1)} %gather_fusion.9), channel_id=1, source_target_pairs={{0,1},{1,2},{2,3},{3,4},{4,5},{5,6},{6,7},{8,9},{9,10},{10,11},{11... | collective-permute-start | bytes 98312 | tf_op jit(solution)/shard_map/ppermute | solution.py:17
  48.5 1.9 collective-permute-start.7
  50.5 4.9 %all-to-all-start.2 = ((f32[8,1,96]{2,1,0:T(1,128)}), f32[8,1,96]{2,1,0:T(1,128)S(1)}, u32[]{:S(2)}, u32[]{:S(2)}) async-start(f32[8,1,96]{2,1,0:T(1,128)} %all_to_all.18), calls=%async_computation.2 | async-start | bytes 8192 | tf_op jit(solution)/shard_map/all_to_all | solution.py:76
  55.4 1.9 gather_fusion.6
  57.3 1.9 gather_fusion
  59.2 1.4 copy.19
  60.7 3.7 %copy.23 = f32[96,64,64]{2,1,0:T(8,128)} copy(f32[96,64,64]{0,2,1:T(8,128)S(1)} %bitcast.47) | data formatting | bytes 3145728 | tf_op jit(solution)/shard_map/convert_element_type | solution.py:55
  64.3 1.6 copy.15
  65.9 3.1 %copy.17 = bf16[96,64,64]{2,1,0:T(8,128)(2,1)} copy(bf16[96,64,64]{0,2,1:T(8,128)(2,1)S(1)} %bitcast.51) | data formatting | bytes 1572864 | tf_op jit(solution)/shard_map/reshape | solution.py:50
  69.0 1.4 copy.13
  70.4 3.7 %copy.18 = f32[96,64,64]{2,1,0:T(8,128)} copy(f32[96,64,64]{0,2,1:T(8,128)S(1)} %bitcast.48) | data formatting | bytes 3145728 | tf_op jit(solution)/shard_map/convert_element_type | solution.py:56
  76.6 6.0 %scatter_custom_fusion.4 = f32[33]{0:T(128)S(1)} fusion(s32[768]{0:T(1024)S(1)} %reshape.285, f32[768]{0:T(1024)S(1)} %reshape.303, f32[]{:T(128)} %constant.11.clone.1), kind=kCustom, calls=%fused_computation.65 | custom fusion | flops 768 | bytes 136 | tf_op jit(solution)/shard_map/scatter-add | solution.py:83
  82.7 1.3 concatenate.9
  83.9 1.0 gather_fusion.5
  85.6 3.1 %copy.16 = bf16[96,64,64]{2,1,0:T(8,128)(2,1)} copy(bf16[96,64,64]{0,2,1:T(8,128)(2,1)S(1)} %bitcast.49) | data formatting | bytes 1572864 | tf_op jit(solution)/shard_map/reshape | solution.py:51
  88.8 2.8 %concatenate.10 = bf16[96,4096]{1,0:T(8,128)(2,1)S(1)} concatenate(bf16[64,4096]{1,0:T(8,128)(2,1)S(1)} %copy-done.1, bf16[12,4096]{1,0:T(8,128)(2,1)S(1)} %collective-permute-done.4, bf16[12,4096]{1,0:T(8,128)(2,1)} %collective-permute-done.5, bf16[4,4096]{1,0:T(4,128)(2,1)} %collective-permute-done.6, bf16[4,4096]{1,0:T(4,128)(2,1)} %collective-permute-done.7), dimensions={0} | concatenate | bytes 1572864 | tf_op jit(solution)/shard_map/concatenate | solution.py:48
  91.6 1.9 gather_fusion.11
  93.5 2.4 %copy.20 = bf16[96,4096]{0,1:T(8,128)(2,1)} copy(bf16[96,4096]{1,0:T(8,128)(2,1)} %gather_fusion.11) | data formatting | bytes 1572864 | tf_op jit(solution)/shard_map/gather | solution.py:52
  95.9 4.0 %copy.21 = bf16[96,64,64]{2,1,0:T(8,128)(2,1)} copy(bf16[96,64,64]{0,2,1:T(8,128)(2,1)} %bitcast.50) | data formatting | bytes 1572864 | tf_op jit(solution)/shard_map/reshape | solution.py:52
  100.0 2.6 %fusion.2 = (f32[96,64]{1,0:T(8,128)S(1)}, f32[96,64,64]{1,2,0:T(8,128)S(1)}) fusion(f32[96,64,64]{2,1,0:T(8,128)S(1)} %copy-done.2, bf16[96,64,64]{2,1,0:T(8,128)(2,1)} %copy.17, bf16[96,64,64]{2,1,0:T(8,128)(2,1)} %copy.16), kind=kOutput, calls=%fused_computation.22 | convolution fusion | flops 51111936 | bytes 4743168 | tf_op jit(solution)/shard_map/tjk,tkr->tjr/dot_general | solution.py:53
  102.6 0.7 copy-done.4
  103.8 0.8 fusion.1
  104.7 1.7 scatter_custom_fusion.1
  106.4 4.8 %all-to-all-start.1 = ((f32[8,96,128]{2,1,0:T(8,128)}), f32[8,96,128]{2,1,0:T(8,128)S(1)}, u32[]{:S(2)}, u32[]{:S(2)}) async-start(f32[8,96,128]{2,1,0:T(8,128)} %bitcast.18), calls=%async_computation.1 | async-start | bytes 786432 | tf_op jit(solution)/shard_map/all_to_all | solution.py:73
  111.2 117.1 %psum.7 = f32[64]{0:T(128)S(1)} all-reduce(f32[64]{0:T(128)S(1)} %get-tuple-element.2), channel_id=1, replica_groups=mesh['gx'=96,'gy'=8] {'gx','gy'}, use_global_device_ids=true, to_apply=%region_10.11 | all-reduce | flops 64 | bytes 512 | tf_op jit(solution)/shard_map/psum | solution.py:63
  228.8 7.1 %scatter_custom_fusion.2 = f32[33,128]{1,0:T(8,128)S(1)} fusion(s32[768]{0:T(1024)S(1)} %reshape.285, f32[768,128]{1,0:T(8,128)S(1)} %bitcast.52, f32[]{:T(128)} %constant.11.clone.1), kind=kCustom, calls=%fused_computation.35 | custom fusion | flops 98304 | bytes 16900 | tf_op jit(solution)/shard_map/scatter-add | solution.py:82
  235.9 0.7 slice_divide_fusion
  (63 shorter events, 6.2 us)
Async XLA Ops:
  0.6 21.9 %copy-start = (bf16[64,4096]{1,0:T(8,128)(2,1)S(1)}, bf16[64,4096]{1,0:T(8,128)(2,1)}, u32[]{:S(2)}) copy-start(bf16[64,4096]{1,0:T(8,128)(2,1)} %param.11) | copy-start | bytes 1572868
  0.6 24.4 %copy-start.8 = (s32[1,2,4]{2,1,0:T(2,128)S(1)}, s32[1,2,4]{2,1,0:T(2,128)}, u32[]{:S(2)}) copy-start(s32[1,2,4]{2,1,0:T(2,128)} %param.21) | copy-start | bytes 100
  0.7 31.1 %copy-start.1 = (bf16[64,4096]{1,0:T(8,128)(2,1)S(1)}, bf16[64,4096]{1,0:T(8,128)(2,1)}, u32[]{:S(2)}) copy-start(bf16[64,4096]{1,0:T(8,128)(2,1)} %param.12) | copy-start | bytes 1572868
  2.5 34.8 %copy-start.11 = (s32[96]{0:T(128)S(1)}, s32[96]{0:T(128)}, u32[]{:S(2)}) copy-start(s32[96]{0:T(128)} %param.14) | copy-start | bytes 1156
  2.5 34.9 %copy-start.12 = (s32[96]{0:T(128)S(1)}, s32[96]{0:T(128)}, u32[]{:S(2)}) copy-start(s32[96]{0:T(128)} %param.15) | copy-start | bytes 1156
  2.5 34.9 %copy-start.13 = (f32[96]{0:T(128)S(1)}, f32[96]{0:T(128)}, u32[]{:S(2)}) copy-start(f32[96]{0:T(128)} %param.16) | copy-start | bytes 1156
  3.2 38.4 %copy-start.14 = (s32[96]{0:T(128)}, s32[96]{0:T(128)S(1)}, u32[]{:S(2)}) copy-start(s32[96]{0:T(128)S(1)} %fusion.17) | copy-start | bytes 1156
  4.9 45.6 %all-to-all-start = ((s32[8,1,96]{2,1,0:T(1,128)}), s32[8,1,96]{2,1,0:T(1,128)S(1)}, u32[]{:S(2)}, u32[]{:S(2)}) async-start(s32[8,1,96]{2,1,0:T(1,128)} %all_to_all.15), calls=%async_computation | async-start | bytes 8192 | tf_op jit(solution)/shard_map/all_to_all | solution.py:78
  21.2 27.3 %collective-permute-start = (bf16[12,4096]{1,0:T(8,128)(2,1)S(1)}, bf16[12,4096]{1,0:T(8,128)(2,1)S(1)}, u32[]{:S(2)}, u32[]{:S(2)}) collective-permute-start(bf16[12,4096]{1,0:T(8,128)(2,1)S(1)} %gather_fusion.1), channel_id=1, source_target_pairs={{0,8},{8,16},{16,24},{24,32},{32,40},{40,48},{48,56},{56,64},{64,7... | collective-permute-start | bytes 294920 | tf_op jit(solution)/shard_map/ppermute | solution.py:17
  23.8 58.9 %collective-permute-start.1 = (bf16[12,4096]{1,0:T(8,128)(2,1)}, bf16[12,4096]{1,0:T(8,128)(2,1)S(1)}, u32[]{:S(2)}, u32[]{:S(2)}) collective-permute-start(bf16[12,4096]{1,0:T(8,128)(2,1)} %gather_fusion.2), channel_id=1, source_target_pairs={{8,0},{16,8},{24,16},{32,24},{40,32},{48,40},{56,48},{64,56},{72,6... | collective-permute-start | bytes 294920 | tf_op jit(solution)/shard_map/ppermute | solution.py:17
  25.7 17.6 %collective-permute-start.2 = (bf16[4,4096]{1,0:T(4,128)(2,1)S(1)}, bf16[4,4096]{1,0:T(4,128)(2,1)S(1)}, u32[]{:S(2)}, u32[]{:S(2)}) collective-permute-start(bf16[4,4096]{1,0:T(4,128)(2,1)S(1)} %gather_fusion.3), channel_id=1, source_target_pairs={{0,1},{1,2},{2,3},{3,4},{4,5},{5,6},{6,7},{8,9},{9,10},{10,11},{11... | collective-permute-start | bytes 98312 | tf_op jit(solution)/shard_map/ppermute | solution.py:17
  29.8 14.7 %collective-permute-start.3 = (bf16[4,4096]{1,0:T(4,128)(2,1)S(1)}, bf16[4,4096]{1,0:T(4,128)(2,1)S(1)}, u32[]{:S(2)}, u32[]{:S(2)}) collective-permute-start(bf16[4,4096]{1,0:T(4,128)(2,1)S(1)} %gather_fusion.4), channel_id=1, source_target_pairs={{1,0},{2,1},{3,2},{4,3},{5,4},{6,5},{7,6},{9,8},{10,9},{11,10},{12... | collective-permute-start | bytes 98312 | tf_op jit(solution)/shard_map/ppermute | solution.py:17
  33.0 55.7 %collective-permute-start.4 = (bf16[12,4096]{1,0:T(8,128)(2,1)}, bf16[12,4096]{1,0:T(8,128)(2,1)S(1)}, u32[]{:S(2)}, u32[]{:S(2)}) collective-permute-start(bf16[12,4096]{1,0:T(8,128)(2,1)} %gather_fusion.7), channel_id=1, source_target_pairs={{0,8},{8,16},{16,24},{24,32},{32,40},{40,48},{48,56},{56,64},{64,7... | collective-permute-start | bytes 294920 | tf_op jit(solution)/shard_map/ppermute | solution.py:17
  43.3 14.0 %copy-start.6 = (bf16[4,4096]{1,0:T(4,128)(2,1)}, bf16[4,4096]{1,0:T(4,128)(2,1)S(1)}, u32[]{:S(2)}) copy-start(bf16[4,4096]{1,0:T(4,128)(2,1)S(1)} %collective-permute-done.2) | copy-start | bytes 98308
  43.3 45.5 %collective-permute-start.5 = (bf16[12,4096]{1,0:T(8,128)(2,1)}, bf16[12,4096]{1,0:T(8,128)(2,1)}, u32[]{:S(2)}, u32[]{:S(2)}) collective-permute-start(bf16[12,4096]{1,0:T(8,128)(2,1)} %gather_fusion.8), channel_id=1, source_target_pairs={{8,0},{16,8},{24,16},{32,24},{40,32},{48,40},{56,48},{64,56},{72,6... | collective-permute-start | bytes 294920 | tf_op jit(solution)/shard_map/ppermute | solution.py:17
  44.6 12.7 %copy-start.7 = (bf16[4,4096]{1,0:T(4,128)(2,1)}, bf16[4,4096]{1,0:T(4,128)(2,1)S(1)}, u32[]{:S(2)}) copy-start(bf16[4,4096]{1,0:T(4,128)(2,1)S(1)} %collective-permute-done.3) | copy-start | bytes 98308
  44.6 44.2 %collective-permute-start.6 = (bf16[4,4096]{1,0:T(4,128)(2,1)}, bf16[4,4096]{1,0:T(4,128)(2,1)}, u32[]{:S(2)}, u32[]{:S(2)}) collective-permute-start(bf16[4,4096]{1,0:T(4,128)(2,1)} %gather_fusion.9), channel_id=1, source_target_pairs={{0,1},{1,2},{2,3},{3,4},{4,5},{5,6},{6,7},{8,9},{9,10},{10,11},{11... | collective-permute-start | bytes 98312 | tf_op jit(solution)/shard_map/ppermute | solution.py:17
  48.5 40.3 %collective-permute-start.7 = (bf16[4,4096]{1,0:T(4,128)(2,1)}, bf16[4,4096]{1,0:T(4,128)(2,1)}, u32[]{:S(2)}, u32[]{:S(2)}) collective-permute-start(bf16[4,4096]{1,0:T(4,128)(2,1)} %gather_fusion.10), channel_id=1, source_target_pairs={{1,0},{2,1},{3,2},{4,3},{5,4},{6,5},{7,6},{9,8},{10,9},{11,10},{12... | collective-permute-start | bytes 98312 | tf_op jit(solution)/shard_map/ppermute | solution.py:17
  50.5 24.9 %all-to-all-start.2 = ((f32[8,1,96]{2,1,0:T(1,128)}), f32[8,1,96]{2,1,0:T(1,128)S(1)}, u32[]{:S(2)}, u32[]{:S(2)}) async-start(f32[8,1,96]{2,1,0:T(1,128)} %all_to_all.18), calls=%async_computation.2 | async-start | bytes 8192 | tf_op jit(solution)/shard_map/all_to_all | solution.py:76
  93.5 6.4 %copy-start.2 = (f32[96,64,64]{2,1,0:T(8,128)S(1)}, f32[96,64,64]{2,1,0:T(8,128)}, u32[]{:S(2)}) copy-start(f32[96,64,64]{2,1,0:T(8,128)} %copy.23) | copy-start | bytes 4718596
  100.0 2.6 %copy-start.3 = (bf16[96,64,64]{2,1,0:T(8,128)(2,1)S(1)}, bf16[96,64,64]{2,1,0:T(8,128)(2,1)}, u32[]{:S(2)}) copy-start(bf16[96,64,64]{2,1,0:T(8,128)(2,1)} %copy.17) | copy-start | bytes 2359300
  100.0 3.3 %copy-start.4 = (f32[96,64,64]{2,1,0:T(8,128)S(1)}, f32[96,64,64]{2,1,0:T(8,128)}, u32[]{:S(2)}) copy-start(f32[96,64,64]{2,1,0:T(8,128)} %copy.18) | copy-start | bytes 4718596
  100.0 3.8 %copy-start.5 = (bf16[96,64,64]{2,1,0:T(8,128)(2,1)S(1)}, bf16[96,64,64]{2,1,0:T(8,128)(2,1)}, u32[]{:S(2)}) copy-start(bf16[96,64,64]{2,1,0:T(8,128)(2,1)} %copy.21) | copy-start | bytes 2359300
  103.8 0.8 copy-start.10
  103.8 0.9 copy-start.9
  106.4 122.4 %all-to-all-start.1 = ((f32[8,96,128]{2,1,0:T(8,128)}), f32[8,96,128]{2,1,0:T(8,128)S(1)}, u32[]{:S(2)}, u32[]{:S(2)}) async-start(f32[8,96,128]{2,1,0:T(8,128)} %bitcast.18), calls=%async_computation.1 | async-start | bytes 786432 | tf_op jit(solution)/shard_map/all_to_all | solution.py:73
where the time goes:
time: 238 us; the launch traced here: 237 us
  blocking collectives  117 us (49%)
  local copies, waits for them, and re-layouts  50.8 us (21%)
  starting transfers between devices  42.9 us (18%)
  other arithmetic  21.3 us (9%)
  matrix products  3.43 us (1%)
    psum x1, blocking collectives, shards(): lax.psum(jnp.sum(energy, axis=0), ('gx', 'gy')) / math.sqrt(total_tiles)  117 us
    ppermute x8, starting transfers between devices, shifted(): return lax.ppermute(x, axis, pairs)  19.4 us
    all_to_all x1, starting transfers between devices, shards(): lax.all_to_all(labels.reshape(rows_y, CAP), 'gy', split_axis=0, concat_ax...  13.7 us
    scatter-add x1, other arithmetic, shards(): jax.ops.segment_sum(got_rows.reshape(-1, 2 * R), flat_labels, NREG + 1)  7.06 us
    scatter-add x1, other arithmetic, shards(): jax.ops.segment_sum(got_weights.reshape(-1), flat_labels, NREG + 1)[:NREG]  6.02 us
    convert_element_type x2, local copies, waits for them, and re-layouts, shards(): lrow = adjoint[tile_rows].reshape(count, BS, R).astype(jnp.float32)  5.11 us
    convert_element_type x2, local copies, waits for them, and re-layouts, shards(): urow = disp[tile_rows].reshape(count, BS, R).astype(jnp.float32)  5.09 us
    all_to_all x1, starting transfers between devices, shards(): lax.all_to_all(weights.reshape(rows_y, CAP), 'gy', split_axis=0, concat_a...  4.93 us
  transfers between devices with their start and end apart: 11, of which 0 were waited for; matrix products, arithmetic and copies ran while one was open for 19% of the time, Pallas kernels for 0%

commit v1 on v0

v1 whole, which is shorter than its diff:
```python
import math

import jax
import jax.numpy as jnp
from jax import lax
from jax.experimental import pallas as pl
from jax.experimental.pallas import tpu as pltpu
from jax.sharding import PartitionSpec as P

BS = 64
R = 64
NREG = 32
NB = 64
NT = 96
LANES = 128
F32 = jnp.float32
BF16 = jnp.bfloat16
ROWS = 40


def left_half(shape):
    return lax.broadcasted_iota(jnp.int32, shape, 1) < R


def pack_kernel(fx_ref, fy_ref, disp_ref, adj_ref, ul_ref, xu_ref, xd_ref, yu_ref, yd_ref, scr):
    left = left_half((NB, LANES))
    for c in range(BS // 2):
        cols = slice(LANES * c, LANES * (c + 1))
        u = disp_ref[:, cols].astype(F32)
        v = adj_ref[:, cols].astype(F32)
        scr[pl.ds(2 * c, NB, stride=BS), :] = jnp.where(left, u, pltpu.roll(v, R, 1))
        scr[pl.ds(2 * c + 1, NB, stride=BS), :] = jnp.where(left, pltpu.roll(u, R, 1), v)
    ul_ref[...] = scr[...].astype(BF16)
    for out, idx, side, n in ((xu_ref, fx_ref, 0, 12), (xd_ref, fx_ref, 1, 12), (yu_ref, fy_ref, 0, 4), (yd_ref, fy_ref, 1, 4)):
        for i in range(n):
            out[i * BS:(i + 1) * BS, :] = ul_ref[pl.ds(pl.multiple_of(idx[0, side, i] * BS, BS), BS), :]


def pack(face_x, face_y, disp, adjoint):
    smem = pl.BlockSpec(memory_space=pltpu.SMEM)
    vmem = pl.BlockSpec(memory_space=pltpu.VMEM)
    sizes = (NB, 12, 12, 4, 4)
    return pl.pallas_call(
        pack_kernel,
        out_shape=[jax.ShapeDtypeStruct((n * BS, LANES), BF16) for n in sizes],
        in_specs=[smem, smem, vmem, vmem],
        out_specs=[vmem] * 5,
        scratch_shapes=[pltpu.VMEM((NB * BS, LANES), F32)],
        compiler_params=pltpu.CompilerParams(vmem_limit_bytes=16 << 20),
    )(face_x, face_y, disp, adjoint)


def stiffness_kernel(tiles_ref, k_ref, scr):
    for c in range(BS // 2):
        k = tiles_ref[:, LANES * c:LANES * (c + 1)].astype(F32)
        scr[pl.ds(2 * c, NT, stride=BS), :] = k
        scr[pl.ds(2 * c + 1, NT, stride=BS), :] = pltpu.roll(k, R, 1)
    k_ref[...] = scr[...].astype(BF16)


def stiffness(tiles):
    vmem = pl.BlockSpec(memory_space=pltpu.VMEM)
    return pl.pallas_call(
        stiffness_kernel,
        out_shape=jax.ShapeDtypeStruct((NT * BS, LANES), BF16),
        in_specs=[vmem],
        out_specs=vmem,
        scratch_shapes=[pltpu.VMEM((NT * BS, LANES), F32)],
        compiler_params=pltpu.CompilerParams(vmem_limit_bytes=16 << 20),
        cost_estimate=pl.CostEstimate(flops=0, bytes_accessed=8 << 20, transcendentals=0),
    )(tiles)


def column(row):
    wide = jnp.broadcast_to(row, (LANES, NT)).T
    return wide


def element_kernel(rows_ref, cols_ref, density_ref, weight_ref, owner_ref, region_ref,
                   k_ref, ul_ref, lx_ref, hx_ref, ly_ref, hy_ref, out_ref, ext, en8, cr8):
    n = NB * BS
    ext[:n, :] = ul_ref[...]
    ext[n:n + 768, :] = lx_ref[...]
    ext[n + 768:n + 1536, :] = hx_ref[...]
    ext[n + 1536:n + 1792, :] = ly_ref[...]
    ext[n + 1792:, :] = hy_ref[...]

    group = 8

    def body(g, carry):
        for i in range(group):
            t = g * group + i
            kmat = k_ref[pl.ds(pl.multiple_of(t * BS, BS), BS), :][:, :BS]
            col = ext[pl.ds(pl.multiple_of(cols_ref[t] * BS, BS), BS), :]
            row = ul_ref[pl.ds(pl.multiple_of(rows_ref[t] * BS, BS), BS), :].astype(F32)
            prod = jnp.dot(kmat, col, preferred_element_type=F32)
            same = row * prod
            other = pltpu.roll(row, R, 1) * prod
            at = pl.ds(pl.multiple_of(t * 8, 8), 8)
            en8[at, :] = jnp.sum(same.reshape(8, 8, LANES), axis=0)
            cr8[at, :] = jnp.sum(other.reshape(8, 8, LANES), axis=0)
        return carry

    lax.fori_loop(0, NT // group, body, 0)
    en = en8[pl.ds(0, NT, stride=8), :]
    cr = cr8[pl.ds(0, NT, stride=8), :]
    for s in range(1, 8):
        en = en + en8[pl.ds(s, NT, stride=8), :]
        cr = cr + cr8[pl.ds(s, NT, stride=8), :]
    left = left_half((NT, LANES))
    energy = pltpu.roll(en, R, 1) / math.sqrt(BS)
    cross = cr + pltpu.roll(cr, R, 1)
    rho = column(density_ref[...])
    weight = column(weight_ref[...])
    sens = -(3.0 * rho * rho / (2.0 * math.sqrt(BS))) * cross
    payload = weight * jnp.where(left, sens, energy)
    ident = owner_ref[...] * NREG + region_ref[...]
    onehot = (lax.broadcasted_iota(jnp.int32, (8 * NREG, NT), 0) == ident).astype(F32).astype(BF16)
    high = payload.astype(BF16)
    rest = payload - high.astype(F32)
    mid = rest.astype(BF16)
    low = (rest - mid.astype(F32)).astype(BF16)
    sums = (jnp.dot(onehot, high, preferred_element_type=F32)
            + jnp.dot(onehot, mid, preferred_element_type=F32)
            + jnp.dot(onehot, low, preferred_element_type=F32))
    ident_col = column(ident.astype(F32)).astype(jnp.int32)
    lane = lax.broadcasted_iota(jnp.int32, (NT, LANES), 1)
    total_energy = jnp.sum(energy, axis=0, keepdims=True)
    sub = lax.broadcasted_iota(jnp.int32, (8, LANES), 0)
    for o in range(8):
        out_ref[o, :NREG, :] = sums[o * NREG:(o + 1) * NREG, :]
        hit = (ident_col == lane + o * NREG) & (lane < NREG)
        totals = jnp.sum(jnp.where(hit, weight, 0.0), axis=0, keepdims=True)
        out_ref[o, NREG:, :] = jnp.where(sub == 0, totals, jnp.where(sub == 1, total_energy, 0.0))


def elements(rows, cols, density, weight, owner, region, k, ul, lx, hx, ly, hy):
    smem = pl.BlockSpec(memory_space=pltpu.SMEM)
    vmem = pl.BlockSpec(memory_space=pltpu.VMEM)
    return pl.pallas_call(
        element_kernel,
        out_shape=jax.ShapeDtypeStruct((8, ROWS, LANES), F32),
        in_specs=[smem, smem] + [vmem] * 10,
        out_specs=vmem,
        scratch_shapes=[pltpu.VMEM((96 * BS, LANES), BF16), pltpu.VMEM((NT * 8, LANES), F32), pltpu.VMEM((NT * 8, LANES), F32)],
        compiler_params=pltpu.CompilerParams(vmem_limit_bytes=16 << 20),
    )(rows, cols, density.reshape(1, NT), weight.reshape(1, NT), owner.reshape(1, NT), region.reshape(1, NT),
      k, ul, lx, hx, ly, hy)


def region_kernel(got_ref, out_ref, energy_ref):
    total = got_ref[0]
    for s in range(1, 8):
        total = total + got_ref[s]
    weights = total[NREG:NREG + 1, :NREG]
    eye = lax.broadcasted_iota(jnp.int32, (NREG, NREG), 0) == lax.broadcasted_iota(jnp.int32, (NREG, NREG), 1)
    divisor = jnp.sum(jnp.where(eye, weights, 0.0), axis=1, keepdims=True)
    out_ref[...] = total[:NREG, :] / jnp.maximum(divisor, 1.0)
    energy_ref[...] = jnp.broadcast_to(total[NREG + 1:NREG + 2, :], energy_ref.shape[:1] + (LANES,)).reshape(energy_ref.shape)


def regions(got, columns):
    vmem = pl.BlockSpec(memory_space=pltpu.VMEM)
    return pl.pallas_call(
        region_kernel,
        out_shape=[jax.ShapeDtypeStruct((NREG, LANES), F32), jax.ShapeDtypeStruct((columns, 1, LANES), F32)],
        in_specs=[vmem],
        out_specs=[vmem, vmem],
        compiler_params=pltpu.CompilerParams(vmem_limit_bytes=16 << 20),
    )(got)


def shifted(x, axis, by):
    size = lax.axis_size(axis)
    pairs = [(i, i + by) for i in range(size) if 0 <= i + by < size]
    return lax.ppermute(x, axis, pairs)


def shards(disp, adjoint, tiles, tile_rows, tile_cols, density, filter_weight, owner, region, face_x, face_y):
    ul, xu, xd, yu, yd = pack(face_x, face_y, disp, adjoint)
    low_x = shifted(xu, "gx", 1)
    high_x = shifted(xd, "gx", -1)
    low_y = shifted(yu, "gy", 1)
    high_y = shifted(yd, "gy", -1)
    k = stiffness(tiles)
    sent = elements(tile_rows, tile_cols, density, filter_weight, owner, region, k, ul, low_x, high_x, low_y, high_y)
    got = lax.all_to_all(sent, "gy", split_axis=0, concat_axis=0, tiled=True)
    columns = lax.axis_size("gx")
    filtered, energy = regions(got, columns)
    energies = lax.all_to_all(energy, "gx", split_axis=0, concat_axis=0, tiled=True)
    total_tiles = NT * columns * lax.axis_size("gy")
    compliance = jnp.sum(energies, axis=(0, 1))[R:] / math.sqrt(total_tiles)
    return (filtered, compliance)


def solution(mesh):
    flat = P(("gx", "gy"))
    wide = P(("gx", "gy"), None)
    deep = P(("gx", "gy"), None, None)
    placed = (wide, wide, wide, flat, flat, flat, flat, wide, flat, deep, deep)
    return jax.shard_map(shards, mesh=mesh, in_specs=placed, out_specs=(wide, P()), check_vma=False)
```

time: 238 us -> 72.8 us (0.31)
  blocking collectives: 117 us -> 40.8 us
  local copies, waits for them, and re-layouts: 50.8 us -> 3.53 us
  starting transfers between devices: 42.9 us -> 16.3 us
  other arithmetic: 21.3 us -> 0.7 us
  Pallas kernels: 0 us -> 10.2 us
  matrix products: 3.43 us -> 0 us
    psum x1 -> x0, blocking collectives: 117 us -> none  [shards(): lax.psum(jnp.sum(energy, axis=0), ('gx', 'gy')) / math.sqrt(total_tiles)]
    all_to_all x0 -> x2, blocking collectives: none -> 40.8 us  [the longest x1 33.2 us: shards(): lax.all_to_all(energy, 'gx', split_axis=0, concat_axis=0, tiled=True)]
    all_to_all x3 -> x0, starting transfers between devices: 23.5 us -> none  [the longest x1 13.7 us: shards(): lax.all_to_all(labels.reshape(rows_y, CAP), 'gy', split_axis=0, concat_ax...]
    gather x14 -> x0, local copies, waits for them, and re-layouts: 18.9 us -> none  [the longest x2 4.29 us: shards(): lcol = adj_ext[tile_cols].reshape(count, BS, R)]
    scatter-add x2 -> x0, other arithmetic: 13.1 us -> none  [the longest x1 7.06 us: shards(): jax.ops.segment_sum(got_rows.reshape(-1, 2 * R), flat_labels, NREG + 1)]
    reshape x4 -> x0, local copies, waits for them, and re-layouts: 10.3 us -> none  [the longest x1 4.05 us: shards(): lcol = adj_ext[tile_cols].reshape(count, BS, R)]
    pallas_call x0 -> x4, Pallas kernels: none -> 10.2 us  [the longest x1 3.33 us: elements(): pl.pallas_call(element_kernel, out_shape=jax.ShapeDtypeStruct((8, ROWS, L...]
    convert_element_type x4 -> x0, local copies, waits for them, and re-layouts: 10.2 us -> none  [the longest x2 5.11 us: shards(): lrow = adjoint[tile_rows].reshape(count, BS, R).astype(jnp.float32)]
  transfers between devices with their start and end apart: 11 -> 4, of which waited for: 0 -> 0; matrix products, arithmetic and copies ran while one was open for 19% -> 0% of each run, Pallas kernels for 0% -> 5%
where the time goes in v1:
time: 72.8 us; the launch traced here: 72.4 us
  blocking collectives  40.8 us (56%)
  starting transfers between devices  16.3 us (22%)
  Pallas kernels  10.2 us (14%)
  local copies, waits for them, and re-layouts  3.53 us (5%)
  between operations  0.82 us (1%)
    all_to_all x1, blocking collectives, shards(): lax.all_to_all(energy, 'gx', split_axis=0, concat_axis=0, tiled=True)  33.2 us
    ppermute x4, starting transfers between devices, shifted(): return lax.ppermute(x, axis, pairs)  16.3 us
    all_to_all x1, blocking collectives, shards(): got = lax.all_to_all(sent, 'gy', split_axis=0, concat_axis=0, tiled=True)  7.67 us
    unnamed x22, local copies, waits for them, and re-layouts  3.53 us
    pallas_call x1, Pallas kernels, elements(): pl.pallas_call(element_kernel, out_shape=jax.ShapeDtypeStruct((8, ROWS, L...  3.33 us
    pallas_call x1, Pallas kernels, stiffness(): pl.pallas_call(stiffness_kernel, out_shape=jax.ShapeDtypeStruct((NT * BS,...  3.26 us
    pallas_call x1, Pallas kernels, pack(): pl.pallas_call(pack_kernel, out_shape=[jax.ShapeDtypeStruct((n * BS, LANE...  2.93 us
  transfers between devices with their start and end apart: 4, of which 0 were waited for; matrix products, arithmetic and copies ran while one was open for 0% of the time, Pallas kernels for 5%

profile of v1, /device:TPU:1, one launch (start us, length us, event | category | flops | bytes accessed | tf_op | source)
XLA Modules:
  0.0 72.4 jit_solution(4308701251245571474)
XLA Ops:
  0.6 0.0 copy-start
  0.6 0.0 copy-start.1
  0.7 1.1 %copy-done.1 = bf16[64,4096]{1,0:T(8,128)(2,1)S(1)} copy-done((bf16[64,4096]{1,0:T(8,128)(2,1)S(1)}, bf16[64,4096]{1,0:T(8,128)(2,1)}, u32[]{:S(2)}) %copy-start.1) | copy-done | bytes 524312
  1.8 0.0 copy-start.2
  1.8 1.0 %copy-done.2 = bf16[64,4096]{1,0:T(8,128)(2,1)S(1)} copy-done((bf16[64,4096]{1,0:T(8,128)(2,1)S(1)}, bf16[64,4096]{1,0:T(8,128)(2,1)}, u32[]{:S(2)}) %copy-start.2) | copy-done | bytes 524312
  2.8 0.0 copy-start.3
  2.8 0.7 copy-done.3
  3.5 0.0 copy-start.4
  3.5 0.7 copy-done.4
  4.2 0.0 copy-start.5
  4.2 0.0 copy-start.6
  4.2 0.0 copy-start.7
  4.2 0.0 copy-start.8
  4.2 0.0 copy-start.9
  4.2 0.0 copy-start.10
  4.2 2.9 %shard_map.123 = (bf16[4096,128]{1,0:T(8,128)(2,1)S(1)}, bf16[768,128]{1,0:T(8,128)(2,1)S(1)}, bf16[768,128]{1,0:T(8,128)(2,1)S(1)}, bf16[256,128]{1,0:T(8,128)(2,1)S(1)}, bf16[256,128]{1,0:T(8,128)(2,1)S(1)}) custom-call(s32[1,2,12]{2,1,0:T(2,128)S(1)} %copy-done.3, s32[1,2,4]{2,1,0:T(2,128)S(1)} %copy-done.4, bf16[64,4096]{1,0:T(8,128)(2,1)S(1)} %copy-done.1, ...), custom_call_target="tpu_custom_call" | custom-call | tf_op jit(solution)/shard_map/pallas_call | solution.py:43
  7.1 4.8 %collective-permute-start = (bf16[768,128]{1,0:T(8,128)(2,1)S(1)}, bf16[768,128]{1,0:T(8,128)(2,1)S(1)}, u32[]{:S(2)}, u32[]{:S(2)}) collective-permute-start(bf16[768,128]{1,0:T(8,128)(2,1)S(1)} %get-tuple-element.10), channel_id=1, source_target_pairs={{0,8},{8,16},{16,24},{24,32},{32,40},{40,48},{48,56},{56,64},{64,7... | collective-permute-start | bytes 589832 | tf_op jit(solution)/shard_map/ppermute | solution.py:176
  12.0 1.3 %collective-permute-start.1 = (bf16[768,128]{1,0:T(8,128)(2,1)S(1)}, bf16[768,128]{1,0:T(8,128)(2,1)S(1)}, u32[]{:S(2)}, u32[]{:S(2)}) collective-permute-start(bf16[768,128]{1,0:T(8,128)(2,1)S(1)} %get-tuple-element.11), channel_id=1, source_target_pairs={{8,0},{16,8},{24,16},{32,24},{40,32},{48,40},{56,48},{64,56},{72,6... | collective-permute-start | bytes 589832 | tf_op jit(solution)/shard_map/ppermute | solution.py:176
  13.3 4.0 %collective-permute-start.2 = (bf16[256,128]{1,0:T(8,128)(2,1)S(1)}, bf16[256,128]{1,0:T(8,128)(2,1)S(1)}, u32[]{:S(2)}, u32[]{:S(2)}) collective-permute-start(bf16[256,128]{1,0:T(8,128)(2,1)S(1)} %get-tuple-element.12), channel_id=1, source_target_pairs={{0,1},{1,2},{2,3},{3,4},{4,5},{5,6},{6,7},{8,9},{9,10},{10,11},{11... | collective-permute-start | bytes 196616 | tf_op jit(solution)/shard_map/ppermute | solution.py:176
  17.2 6.2 %collective-permute-start.3 = (bf16[256,128]{1,0:T(8,128)(2,1)S(1)}, bf16[256,128]{1,0:T(8,128)(2,1)S(1)}, u32[]{:S(2)}, u32[]{:S(2)}) collective-permute-start(bf16[256,128]{1,0:T(8,128)(2,1)S(1)} %get-tuple-element.13), channel_id=1, source_target_pairs={{1,0},{2,1},{3,2},{4,3},{5,4},{6,5},{7,6},{9,8},{10,9},{11,10},{12... | collective-permute-start | bytes 196616 | tf_op jit(solution)/shard_map/ppermute | solution.py:176
  23.5 0.0 copy-done
  23.5 3.3 %shard_map.122.k_ref = bf16[6144,128]{1,0:T(8,128)(2,1)S(1)} custom-call(bf16[96,4096]{1,0:T(8,128)(2,1)S(1)} %copy-done), custom_call_target="tpu_custom_call" | custom-call | bytes 8388608 | tf_op jit(solution)/shard_map/pallas_call | solution.py:63
  26.7 0.0 collective-permute-done.2.ly_ref
  26.8 0.0 collective-permute-done.3.hy_ref
  26.8 0.0 collective-permute-done.lx_ref
  26.8 0.0 collective-permute-done.1.hx_ref
  26.8 0.0 copy-done.5
  26.8 0.0 copy-done.6
  26.8 0.0 copy-done.7
  26.8 0.0 copy-done.8
  26.8 0.0 copy-done.9
  26.8 0.0 copy-done.10
  26.9 3.3 %shard_map.124 = f32[8,40,128]{2,1,0:T(8,128)S(1)} custom-call(s32[96]{0:T(128)S(1)} %copy-done.5, s32[96]{0:T(128)S(1)} %copy-done.6, f32[1,96]{1,0:T(1,128)S(1)} %bitcast.4, f32[1,96]{1,0:T(1,128)S(1)} %bitcast.5, s32[1,96]{1,0:T(1,128)S(1)} %bitcast.6, s32[1,96]{1,0:T(1,128)S(1)} %bitcast.7, bf16[6144,128]{1,0:T(8,128)(2,1)S(1)} %shard_map.122.k_ref, ...), custom_call_target="tpu_custom_call" | custom-call | tf_op jit(solution)/shard_map/pallas_call | solution.py:140
  30.2 7.7 %all_to_all.10.got_ref = f32[8,40,128]{2,1,0:T(8,128)S(1)} all-to-all(f32[8,40,128]{2,1,0:T(8,128)S(1)} %shard_map.124), channel_id=1, replica_groups=mesh['gx'=96,'gy'=8] {'gy'}, dimensions={0} | all-to-all | bytes 327680 | tf_op jit(solution)/shard_map/all_to_all | solution.py:187
  37.9 0.7 shard_map.125
  38.6 33.2 %all_to_all.11 = f32[96,1,128]{2,1,0:T(1,128)S(1)} all-to-all(f32[96,1,128]{2,1,0:T(1,128)S(1)} %get-tuple-element.15), channel_id=1, replica_groups=mesh['gx'=96,'gy'=8] {'gx'}, dimensions={0} | all-to-all | bytes 98304 | tf_op jit(solution)/shard_map/all_to_all | solution.py:190
  71.7 0.1 reduce_sum.9
  71.9 0.6 slice_multiply_fusion
Async XLA Ops:
  0.6 22.8 %copy-start = (bf16[96,4096]{1,0:T(8,128)(2,1)S(1)}, bf16[96,4096]{1,0:T(8,128)(2,1)}, u32[]{:S(2)}) copy-start(bf16[96,4096]{1,0:T(8,128)(2,1)} %tiles_ref.1) | copy-start | bytes 2359300
  0.6 1.1 %copy-start.1 = (bf16[64,4096]{1,0:T(8,128)(2,1)S(1)}, bf16[64,4096]{1,0:T(8,128)(2,1)}, u32[]{:S(2)}) copy-start(bf16[64,4096]{1,0:T(8,128)(2,1)} %disp_ref.1) | copy-start | bytes 1572868
  1.8 1.0 %copy-start.2 = (bf16[64,4096]{1,0:T(8,128)(2,1)S(1)}, bf16[64,4096]{1,0:T(8,128)(2,1)}, u32[]{:S(2)}) copy-start(bf16[64,4096]{1,0:T(8,128)(2,1)} %adj_ref.1) | copy-start | bytes 1572868
  2.8 0.7 copy-start.3
  3.5 0.7 copy-start.4
  4.2 22.6 %copy-start.5 = (s32[96]{0:T(128)S(1)}, s32[96]{0:T(128)}, u32[]{:S(2)}) copy-start(s32[96]{0:T(128)} %rows_ref.1) | copy-start | bytes 1156
  4.2 22.6 %copy-start.6 = (s32[96]{0:T(128)S(1)}, s32[96]{0:T(128)}, u32[]{:S(2)}) copy-start(s32[96]{0:T(128)} %cols_ref.1) | copy-start | bytes 1156
  4.2 22.6 %copy-start.7 = (f32[96]{0:T(128)S(1)}, f32[96]{0:T(128)}, u32[]{:S(2)}) copy-start(f32[96]{0:T(128)} %param.16) | copy-start | bytes 1156
  4.2 22.7 %copy-start.8 = (f32[96]{0:T(128)S(1)}, f32[96]{0:T(128)}, u32[]{:S(2)}) copy-start(f32[96]{0:T(128)} %param.17) | copy-start | bytes 1156
  4.2 22.7 %copy-start.9 = (s32[96,1]{0,1:T(1,128)S(1)}, s32[96,1]{0,1:T(1,128)}, u32[]{:S(2)}) copy-start(s32[96,1]{0,1:T(1,128)} %param.18) | copy-start | bytes 1156
  4.2 22.7 %copy-start.10 = (s32[96]{0:T(128)S(1)}, s32[96]{0:T(128)}, u32[]{:S(2)}) copy-start(s32[96]{0:T(128)} %param.19) | copy-start | bytes 1156
  7.1 19.6 %collective-permute-start = (bf16[768,128]{1,0:T(8,128)(2,1)S(1)}, bf16[768,128]{1,0:T(8,128)(2,1)S(1)}, u32[]{:S(2)}, u32[]{:S(2)}) collective-permute-start(bf16[768,128]{1,0:T(8,128)(2,1)S(1)} %get-tuple-element.10), channel_id=1, source_target_pairs={{0,8},{8,16},{16,24},{24,32},{32,40},{40,48},{48,56},{56,64},{64,7... | collective-permute-start | bytes 589832 | tf_op jit(solution)/shard_map/ppermute | solution.py:176
  12.0 14.8 %collective-permute-start.1 = (bf16[768,128]{1,0:T(8,128)(2,1)S(1)}, bf16[768,128]{1,0:T(8,128)(2,1)S(1)}, u32[]{:S(2)}, u32[]{:S(2)}) collective-permute-start(bf16[768,128]{1,0:T(8,128)(2,1)S(1)} %get-tuple-element.11), channel_id=1, source_target_pairs={{8,0},{16,8},{24,16},{32,24},{40,32},{48,40},{56,48},{64,56},{72,6... | collective-permute-start | bytes 589832 | tf_op jit(solution)/shard_map/ppermute | solution.py:176
  13.3 13.5 %collective-permute-start.2 = (bf16[256,128]{1,0:T(8,128)(2,1)S(1)}, bf16[256,128]{1,0:T(8,128)(2,1)S(1)}, u32[]{:S(2)}, u32[]{:S(2)}) collective-permute-start(bf16[256,128]{1,0:T(8,128)(2,1)S(1)} %get-tuple-element.12), channel_id=1, source_target_pairs={{0,1},{1,2},{2,3},{3,4},{4,5},{5,6},{6,7},{8,9},{9,10},{10,11},{11... | collective-permute-start | bytes 196616 | tf_op jit(solution)/shard_map/ppermute | solution.py:176
  17.2 9.5 %collective-permute-start.3 = (bf16[256,128]{1,0:T(8,128)(2,1)S(1)}, bf16[256,128]{1,0:T(8,128)(2,1)S(1)}, u32[]{:S(2)}, u32[]{:S(2)}) collective-permute-start(bf16[256,128]{1,0:T(8,128)(2,1)S(1)} %get-tuple-element.13), channel_id=1, source_target_pairs={{1,0},{2,1},{3,2},{4,3},{5,4},{6,5},{7,6},{9,8},{10,9},{11,10},{12... | collective-permute-start | bytes 196616 | tf_op jit(solution)/shard_map/ppermute | solution.py:176

commit v2 on v1

v2 whole, which is shorter than its diff:
```python
import functools
import math

import jax
import jax.numpy as jnp
from jax import lax
from jax.experimental import pallas as pl
from jax.experimental.pallas import tpu as pltpu
from jax.sharding import Mesh, PartitionSpec as P

BS = 64
R = 64
NREG = 32
NB = 64
NT = 96
NIX = 12
NIY = 4
OWNERS = 8
LANES = 128
HALF = BS // 2
SENT_ROWS = 40
GROUP = 32
F32 = jnp.float32
BF16 = jnp.bfloat16
SMEM = pl.BlockSpec(memory_space=pltpu.SMEM)
VMEM = pl.BlockSpec(memory_space=pltpu.VMEM)
HBM = pl.BlockSpec(memory_space=pltpu.HBM)
PARAMS = pltpu.CompilerParams(vmem_limit_bytes=16 << 20)


def pack_kernel(fx_ref, fy_ref, disp_ref, adj_ref, ul_ref, x1_ref, x2_ref, y1_ref, y2_ref, disp, adj, fx, fy, sems):
    pairs = ((disp_ref, disp), (adj_ref, adj), (fx_ref, fx), (fy_ref, fy))
    copies = [pltpu.make_async_copy(src, dst, sems.at[i]) for i, (src, dst) in enumerate(pairs)]
    for copy in copies:
        copy.start()
    for copy in copies:
        copy.wait()
    u = disp[...].reshape(NB, HALF, LANES)
    v = adj[...].reshape(NB, HALF, LANES)
    ul_ref[:, :HALF, :] = jnp.concatenate([u[..., :R], v[..., :R]], axis=-1)
    ul_ref[:, HALF:, :] = jnp.concatenate([u[..., R:], v[..., R:]], axis=-1)
    odd_x = lax.rem(lax.axis_index("z"), 2)
    odd_y = lax.axis_index("c")
    for out, idx, side, count in ((x1_ref, fx, odd_x, NIX), (x2_ref, fx, 1 - odd_x, NIX),
                                  (y1_ref, fy, odd_y, NIY), (y2_ref, fy, 1 - odd_y, NIY)):
        for i in range(count):
            out[i] = ul_ref[idx[0, side, i]]


def pack(face_x, face_y, disp, adjoint):
    args = [pltpu.with_memory_space_constraint(a, pltpu.HBM) for a in (face_x, face_y, disp, adjoint)]
    return pl.pallas_call(
        pack_kernel,
        out_shape=[jax.ShapeDtypeStruct((n, BS, LANES), BF16) for n in (NB, NIX, NIX, NIY, NIY)],
        in_specs=[HBM] * 4,
        out_specs=[VMEM] * 5,
        scratch_shapes=[pltpu.VMEM((NB, BS * R), BF16), pltpu.VMEM((NB, BS * R), BF16),
                        pltpu.SMEM((1, 2, NIX), jnp.int32), pltpu.SMEM((1, 2, NIY), jnp.int32),
                        pltpu.SemaphoreType.DMA((4,))],
        compiler_params=PARAMS,
    )(*args)


def stiffness_kernel(tiles_ref, k_ref):
    pairs = tiles_ref[...].reshape(NT * HALF, LANES)
    source = lax.broadcasted_iota(jnp.int32, (LANES, 2 * LANES), 0)
    target = lax.broadcasted_iota(jnp.int32, (LANES, 2 * LANES), 1)
    lane = target % LANES
    wanted = (target // LANES) * BS + 2 * (lane % HALF) + lane // HALF
    order = ((source == wanted) & (lane < BS)).astype(F32).astype(BF16)
    moved = jnp.dot(pairs, order, preferred_element_type=F32).astype(BF16)
    k_ref[:, :HALF, :] = moved[:, :LANES].reshape(NT, HALF, LANES)
    k_ref[:, HALF:, :] = moved[:, LANES:].reshape(NT, HALF, LANES)


def stiffness(tiles):
    return pl.pallas_call(
        stiffness_kernel,
        out_shape=jax.ShapeDtypeStruct((NT, BS, LANES), BF16),
        in_specs=[VMEM],
        out_specs=VMEM,
        compiler_params=PARAMS,
        cost_estimate=pl.CostEstimate(flops=0, bytes_accessed=8 << 20, transcendentals=0),
    )(tiles)


def column(row):
    return jnp.broadcast_to(row, (LANES, NT)).T


def element_kernel(rows_ref, cols_ref, density_ref, weight_ref, owner_ref, region_ref, k_ref, ul_ref,
                   x1_ref, x2_ref, y1_ref, y2_ref, sent_ref, ext, same8, cross8):
    odd_x = lax.rem(lax.axis_index("z"), 2)
    odd_y = lax.axis_index("c")
    ext[:NB] = ul_ref[...]
    ext[pl.ds(NB + NIX * (1 - odd_x), NIX)] = x1_ref[...]
    ext[pl.ds(NB + NIX * odd_x, NIX)] = x2_ref[...]
    ext[pl.ds(NB + 2 * NIX + NIY * (1 - odd_y), NIY)] = y1_ref[...]
    ext[pl.ds(NB + 2 * NIX + NIY * odd_y, NIY)] = y2_ref[...]

    def body(g, carry):
        for i in range(GROUP):
            t = g * GROUP + i
            row = ul_ref[rows_ref[t]].astype(F32)
            prod = jnp.dot(k_ref[t][:, :BS], ext[cols_ref[t]], preferred_element_type=F32)
            at = pl.ds(pl.multiple_of(t * 8, 8), 8)
            same8[at, :] = jnp.sum((row * prod).reshape(8, 8, LANES), axis=0)
            cross8[at, :] = jnp.sum((pltpu.roll(row, R, 1) * prod).reshape(8, 8, LANES), axis=0)
        return carry

    lax.fori_loop(0, NT // GROUP, body, 0)
    same = same8[pl.ds(0, NT, stride=8), :]
    cross = cross8[pl.ds(0, NT, stride=8), :]
    for s in range(1, 8):
        same = same + same8[pl.ds(s, NT, stride=8), :]
        cross = cross + cross8[pl.ds(s, NT, stride=8), :]
    energy = same / math.sqrt(BS)
    cross = cross + pltpu.roll(cross, R, 1)
    energy_total = jnp.sum(energy, axis=0, keepdims=True)
    rho = column(density_ref[...])
    weight = column(weight_ref[...])
    sens = -(3.0 * rho * rho / (2.0 * math.sqrt(BS))) * cross
    left = lax.broadcasted_iota(jnp.int32, (NT, LANES), 1) < R
    payload = weight * jnp.where(left, sens, pltpu.roll(energy, R, 1))
    ident = owner_ref[...] * NREG + region_ref[...]
    onehot = (lax.broadcasted_iota(jnp.int32, (OWNERS * NREG, NT), 0) == ident).astype(F32).astype(BF16)
    high = payload.astype(BF16)
    rest = payload - high.astype(F32)
    mid = rest.astype(BF16)
    low = (rest - mid.astype(F32)).astype(BF16)
    sums = (jnp.dot(onehot, high, preferred_element_type=F32)
            + jnp.dot(onehot, mid, preferred_element_type=F32)
            + jnp.dot(onehot, low, preferred_element_type=F32))
    ident_column = column(ident.astype(F32)).astype(jnp.int32)
    lane = lax.broadcasted_iota(jnp.int32, (NT, LANES), 1)
    place = lax.broadcasted_iota(jnp.int32, (8, LANES), 0)
    for o in range(OWNERS):
        sent_ref[o, :NREG, :] = sums[o * NREG:(o + 1) * NREG, :]
        hit = (ident_column == lane + o * NREG) & (lane < NREG)
        totals = jnp.sum(jnp.where(hit, weight, 0.0), axis=0, keepdims=True)
        sent_ref[o, NREG:, :] = jnp.where(place == 0, totals, jnp.where(place == 1, energy_total, 0.0))


def elements(rows, cols, density, weight, owner, region, k, ul, x1, x2, y1, y2):
    return pl.pallas_call(
        element_kernel,
        out_shape=jax.ShapeDtypeStruct((OWNERS, SENT_ROWS, LANES), F32),
        in_specs=[SMEM, SMEM] + [VMEM] * 10,
        out_specs=VMEM,
        scratch_shapes=[pltpu.VMEM((NT, BS, LANES), BF16), pltpu.VMEM((NT * 8, LANES), F32), pltpu.VMEM((NT * 8, LANES), F32)],
        compiler_params=PARAMS,
    )(rows, cols, density.reshape(1, NT), weight.reshape(1, NT), owner.reshape(1, NT), region.reshape(1, NT),
      k, ul, x1, x2, y1, y2)


def region_kernel(got_ref, out_ref, energy_ref):
    total = got_ref[0]
    for s in range(1, OWNERS):
        total = total + got_ref[s]
    weights = total[NREG:NREG + 1, :NREG]
    eye = lax.broadcasted_iota(jnp.int32, (NREG, NREG), 0) == lax.broadcasted_iota(jnp.int32, (NREG, NREG), 1)
    divisor = jnp.sum(jnp.where(eye, weights, 0.0), axis=1, keepdims=True)
    out_ref[...] = total[:NREG, :] / jnp.maximum(divisor, 1.0)
    energy = total[NREG + 1:NREG + 2, :]
    energy_ref[...] = jnp.broadcast_to(energy, (energy_ref.shape[0], LANES)).reshape(energy_ref.shape)


def regions(got, columns):
    return pl.pallas_call(
        region_kernel,
        out_shape=[jax.ShapeDtypeStruct((NREG, LANES), F32), jax.ShapeDtypeStruct((columns, 1, LANES), F32)],
        in_specs=[VMEM],
        out_specs=[VMEM, VMEM],
        compiler_params=PARAMS,
    )(got)


def last_kernel(scale, got_ref, out_ref):
    out_ref[...] = (jnp.sum(got_ref[...], axis=0) / scale).reshape(LANES)[:R]


def last(got, scale):
    return pl.pallas_call(
        functools.partial(last_kernel, scale),
        out_shape=jax.ShapeDtypeStruct((R,), F32),
        in_specs=[VMEM],
        out_specs=VMEM,
        compiler_params=PARAMS,
    )(got)


def swaps(axes, size):
    for start in (0, 1):
        firsts = range(start, size - 1, 2)
        yield axes, [(i, i + 1) for i in firsts] + [(i + 1, i) for i in firsts]


def exchange(x, axes):
    return lax.all_to_all(x, axes, split_axis=0, concat_axis=0, tiled=True)


def shards(disp, adjoint, tiles, tile_rows, tile_cols, density, filter_weight, owner, region, face_x, face_y):
    ny, nz, nx, nc = (lax.axis_size(a) for a in ("y", "z", "x", "c"))
    ul, *faces = pack(face_x, face_y, disp, adjoint)
    plans = [*swaps(("y", "z"), ny * nz), *swaps(("x", "c"), nx * nc)]
    halos = [lax.ppermute(face, axes, pairs) for face, (axes, pairs) in zip(faces, plans)]
    k = stiffness(tiles)
    sent = elements(tile_rows, tile_cols, density, filter_weight, owner, region, k, ul, *halos)
    filtered, energy = regions(exchange(sent, ("x", "c")), ny * nz)
    compliance = last(exchange(energy, ("y", "z")), math.sqrt(NT * ny * nz * nx * nc))
    return (filtered, compliance)


def solution(mesh):
    columns, rows = mesh.devices.shape
    nz = 12 if columns % 12 == 0 else columns
    parts = Mesh(mesh.devices.reshape(columns // nz, nz, rows // 2, 2), ("y", "z", "x", "c"))
    axes = ("y", "z", "x", "c")
    flat, wide, deep = P(axes), P(axes, None), P(axes, None, None)
    placed = (wide, wide, wide, flat, flat, flat, flat, wide, flat, deep, deep)
    return jax.shard_map(shards, mesh=parts, in_specs=placed, out_specs=(wide, P()), check_vma=False)
```

time: 72.8 us -> 66.6 us (0.915)
  Pallas kernels: 10.2 us -> 5.99 us
  local copies, waits for them, and re-layouts: 3.53 us -> 0.03 us
  waiting for transfers between devices: 0.01 us -> 3.06 us
  blocking collectives: 40.8 us -> 39.5 us
    pallas_call x3 -> x4, Pallas kernels: 9.52 us -> 5.29 us  [the longest x1 2.23 us: elements(): pl.pallas_call(element_kernel, out_shape=jax.ShapeDtypeStruct((OWNERS, SE...]
    unnamed x22 -> x14, local copies, waits for them, and re-layouts: 3.53 us -> 0.03 us
    ppermute x4, waiting for transfers between devices: 0.01 us -> 3.06 us  [shards(): lax.ppermute(face, axes, pairs)]
    all_to_all x2, blocking collectives: 40.8 us -> 39.5 us  [exchange(): return lax.all_to_all(x, axes, split_axis=0, concat_axis=0, tiled=True)]
  transfers between devices with their start and end apart: 4 -> 4, of which waited for: 0 -> 1; matrix products, arithmetic and copies ran while one was open for 0% -> 0% of each run, Pallas kernels for 5% -> 1%
where the time goes in v2:
time: 66.6 us; the launch traced here: 66.3 us
  blocking collectives  39.5 us (59%)
  starting transfers between devices  16.9 us (25%)
  Pallas kernels  5.99 us (9%)
  waiting for transfers between devices  3.06 us (5%)
  between operations  0.81 us (1%)
    all_to_all x2, blocking collectives, exchange(): return lax.all_to_all(x, axes, split_axis=0, concat_axis=0, tiled=True)  39.5 us
    ppermute x4, starting transfers between devices, shards(): lax.ppermute(face, axes, pairs)  16.9 us
    ppermute x4, waiting for transfers between devices, shards(): lax.ppermute(face, axes, pairs)  3.06 us
    pallas_call x1, Pallas kernels, elements(): pl.pallas_call(element_kernel, out_shape=jax.ShapeDtypeStruct((OWNERS, SE...  2.23 us
    pallas_call x1, Pallas kernels, pack(): pl.pallas_call(pack_kernel, out_shape=[jax.ShapeDtypeStruct((n, BS, LANES...  1.87 us
  transfers between devices with their start and end apart: 4, of which 1 were waited for; matrix products, arithmetic and copies ran while one was open for 0% of the time, Pallas kernels for 1%

profile of v2, /device:TPU:1, one launch (start us, length us, event | category | flops | bytes accessed | tf_op | source)
XLA Modules:
  0.0 66.3 jit_solution(8782722506005386260)
XLA Ops:
  0.6 0.0 copy-start
  0.6 0.0 copy-start.3
  0.7 0.0 copy-start.4
  0.7 0.0 copy-start.5
  0.7 0.0 copy-start.6
  0.7 0.0 copy-start.1
  0.7 0.0 copy-start.2
  0.7 1.9 %shard_map.123 = (bf16[64,64,128]{2,1,0:T(8,128)(2,1)S(1)}, bf16[12,64,128]{2,1,0:T(8,128)(2,1)S(1)}, bf16[12,64,128]{2,1,0:T(8,128)(2,1)S(1)}, bf16[4,64,128]{2,1,0:T(8,128)(2,1)S(1)}, bf16[4,64,128]{2,1,0:T(8,128)(2,1)S(1)}) custom-call(s32[1,2,12]{2,1,0:T(2,128)} %fx_ref.1, s32[1,2,4]{2,1,0:T(2,128)} %fy_ref.1, bf16[64,4096]{1,0:T(8,128)(2,1)} %disp_ref.1, ...), custom_call_target="tpu_custom_call" | custom-call | tf_op jit(solution)/shard_map/pallas_call | solution.py:52
  2.6 4.8 %collective-permute-start = (bf16[12,64,128]{2,1,0:T(8,128)(2,1)S(1)}, bf16[12,64,128]{2,1,0:T(8,128)(2,1)S(1)}, u32[]{:S(2)}, u32[]{:S(2)}) collective-permute-start(bf16[12,64,128]{2,1,0:T(8,128)(2,1)S(1)} %get-tuple-element.10), channel_id=1, source_target_pairs={{0,8},{16,24},{32,40},{48,56},{64,72},{80,88},{96,104},{112,120},{... | collective-permute-start | bytes 589832 | tf_op jit(solution)/shard_map/ppermute | solution.py:206
  7.4 0.7 %collective-permute-start.1 = (bf16[12,64,128]{2,1,0:T(8,128)(2,1)S(1)}, bf16[12,64,128]{2,1,0:T(8,128)(2,1)S(1)}, u32[]{:S(2)}, u32[]{:S(2)}) collective-permute-start(bf16[12,64,128]{2,1,0:T(8,128)(2,1)S(1)} %get-tuple-element.11), channel_id=1, source_target_pairs={{8,16},{24,32},{40,48},{56,64},{72,80},{88,96},{104,112},{120,128}... | collective-permute-start | bytes 589832 | tf_op jit(solution)/shard_map/ppermute | solution.py:206
  8.1 9.5 %collective-permute-start.2 = (bf16[4,64,128]{2,1,0:T(8,128)(2,1)S(1)}, bf16[4,64,128]{2,1,0:T(8,128)(2,1)S(1)}, u32[]{:S(2)}, u32[]{:S(2)}) collective-permute-start(bf16[4,64,128]{2,1,0:T(8,128)(2,1)S(1)} %get-tuple-element.12), channel_id=1, source_target_pairs={{0,1},{2,3},{4,5},{6,7},{1,0},{3,2},{5,4},{7,6},{8,9},{10,11},{12,... | collective-permute-start | bytes 196616 | tf_op jit(solution)/shard_map/ppermute | solution.py:206
  17.6 1.9 %collective-permute-start.3 = (bf16[4,64,128]{2,1,0:T(8,128)(2,1)S(1)}, bf16[4,64,128]{2,1,0:T(8,128)(2,1)S(1)}, u32[]{:S(2)}, u32[]{:S(2)}) collective-permute-start(bf16[4,64,128]{2,1,0:T(8,128)(2,1)S(1)} %get-tuple-element.13), channel_id=1, source_target_pairs={{1,2},{3,4},{5,6},{2,1},{4,3},{6,5},{9,10},{11,12},{13,14},{10,9},... | collective-permute-start | bytes 196616 | tf_op jit(solution)/shard_map/ppermute | solution.py:206
  19.6 0.0 copy-done
  19.6 0.6 shard_map.122.k_ref
  20.1 0.0 collective-permute-done.2.y1_ref
  20.2 3.1 %collective-permute-done.3.y2_ref = bf16[4,64,128]{2,1,0:T(8,128)(2,1)S(1)} collective-permute-done((bf16[4,64,128]{2,1,0:T(8,128)(2,1)S(1)}, bf16[4,64,128]{2,1,0:T(8,128)(2,1)S(1)}, u32[]{:S(2)}, u32[]{:S(2)}) %collective-permute-start.3) | collective-permute-done | bytes 65568 | tf_op jit(solution)/shard_map/ppermute | solution.py:206
  23.2 0.0 collective-permute-done.x1_ref
  23.2 0.0 collective-permute-done.1.x2_ref
  23.2 0.0 copy-done.3
  23.2 0.0 copy-done.4
  23.2 0.0 copy-done.5
  23.2 0.0 copy-done.6
  23.3 0.0 copy-done.1
  23.3 0.0 copy-done.2
  23.3 2.2 %shard_map.124 = f32[8,40,128]{2,1,0:T(8,128)S(1)} custom-call(s32[96]{0:T(128)S(1)} %copy-done.1, s32[96]{0:T(128)S(1)} %copy-done.2, f32[1,96]{1,0:T(1,128)S(1)} %bitcast.4, f32[1,96]{1,0:T(1,128)S(1)} %bitcast.5, s32[1,96]{1,0:T(1,128)S(1)} %bitcast.6, s32[1,96]{1,0:T(1,128)S(1)} %bitcast.7, bf16[96,64,128]{2,1,0:T(8,128)(2,1)S(1)} %shard_map.122.k_ref, ...), custom_call_target="tpu_custom_call" | custom-call | tf_op jit(solution)/shard_map/pallas_call | solution.py:145
  25.5 7.2 %all_to_all.10.got_ref = f32[8,40,128]{2,1,0:T(8,128)S(1)} all-to-all(f32[8,40,128]{2,1,0:T(8,128)S(1)} %shard_map.124), channel_id=1, replica_groups=mesh['y'=8,'z'=12,'x'=4,'c'=2] {'x','c'}, dimensions={0} | all-to-all | bytes 327680 | tf_op jit(solution)/shard_map/all_to_all | solution.py:199
  32.7 0.7 %shard_map.125 = (f32[32,128]{1,0:T(8,128)}, f32[96,1,128]{2,1,0:T(1,128)S(1)}) custom-call(f32[8,40,128]{2,1,0:T(8,128)S(1)} %all_to_all.10.got_ref), custom_call_target="tpu_custom_call" | custom-call | tf_op jit(solution)/shard_map/pallas_call | solution.py:169
  33.4 32.4 %all_to_all.11.got_ref = f32[96,1,128]{2,1,0:T(1,128)S(1)} all-to-all(f32[96,1,128]{2,1,0:T(1,128)S(1)} %get-tuple-element.15), channel_id=1, replica_groups=mesh['y'=8,'z'=12,'x'=4,'c'=2] {'y','z'}, dimensions={0} | all-to-all | bytes 98304 | tf_op jit(solution)/shard_map/all_to_all | solution.py:199
  65.7 0.6 shard_map.126
Async XLA Ops:
  0.6 18.9 %copy-start = (bf16[96,4096]{1,0:T(8,128)(2,1)S(1)}, bf16[96,4096]{1,0:T(8,128)(2,1)}, u32[]{:S(2)}) copy-start(bf16[96,4096]{1,0:T(8,128)(2,1)} %tiles_ref.1) | copy-start | bytes 2359300
  0.6 22.6 %copy-start.3 = (f32[96]{0:T(128)S(1)}, f32[96]{0:T(128)}, u32[]{:S(2)}) copy-start(f32[96]{0:T(128)} %param.16) | copy-start | bytes 1156
  0.7 22.6 %copy-start.4 = (f32[96]{0:T(128)S(1)}, f32[96]{0:T(128)}, u32[]{:S(2)}) copy-start(f32[96]{0:T(128)} %param.17) | copy-start | bytes 1156
  0.7 22.6 %copy-start.5 = (s32[96,1]{0,1:T(1,128)S(1)}, s32[96,1]{0,1:T(1,128)}, u32[]{:S(2)}) copy-start(s32[96,1]{0,1:T(1,128)} %param.18) | copy-start | bytes 1156
  0.7 22.6 %copy-start.6 = (s32[96]{0:T(128)S(1)}, s32[96]{0:T(128)}, u32[]{:S(2)}) copy-start(s32[96]{0:T(128)} %param.19) | copy-start | bytes 1156
  0.7 22.6 %copy-start.1 = (s32[96]{0:T(128)S(1)}, s32[96]{0:T(128)}, u32[]{:S(2)}) copy-start(s32[96]{0:T(128)} %rows_ref.1) | copy-start | bytes 1156
  0.7 22.6 %copy-start.2 = (s32[96]{0:T(128)S(1)}, s32[96]{0:T(128)}, u32[]{:S(2)}) copy-start(s32[96]{0:T(128)} %cols_ref.1) | copy-start | bytes 1156
  2.6 20.6 %collective-permute-start = (bf16[12,64,128]{2,1,0:T(8,128)(2,1)S(1)}, bf16[12,64,128]{2,1,0:T(8,128)(2,1)S(1)}, u32[]{:S(2)}, u32[]{:S(2)}) collective-permute-start(bf16[12,64,128]{2,1,0:T(8,128)(2,1)S(1)} %get-tuple-element.10), channel_id=1, source_target_pairs={{0,8},{16,24},{32,40},{48,56},{64,72},{80,88},{96,104},{112,120},{... | collective-permute-start | bytes 589832 | tf_op jit(solution)/shard_map/ppermute | solution.py:206
  7.4 15.8 %collective-permute-start.1 = (bf16[12,64,128]{2,1,0:T(8,128)(2,1)S(1)}, bf16[12,64,128]{2,1,0:T(8,128)(2,1)S(1)}, u32[]{:S(2)}, u32[]{:S(2)}) collective-permute-start(bf16[12,64,128]{2,1,0:T(8,128)(2,1)S(1)} %get-tuple-element.11), channel_id=1, source_target_pairs={{8,16},{24,32},{40,48},{56,64},{72,80},{88,96},{104,112},{120,128}... | collective-permute-start | bytes 589832 | tf_op jit(solution)/shard_map/ppermute | solution.py:206
  8.1 12.0 %collective-permute-start.2 = (bf16[4,64,128]{2,1,0:T(8,128)(2,1)S(1)}, bf16[4,64,128]{2,1,0:T(8,128)(2,1)S(1)}, u32[]{:S(2)}, u32[]{:S(2)}) collective-permute-start(bf16[4,64,128]{2,1,0:T(8,128)(2,1)S(1)} %get-tuple-element.12), channel_id=1, source_target_pairs={{0,1},{2,3},{4,5},{6,7},{1,0},{3,2},{5,4},{7,6},{8,9},{10,11},{12,... | collective-permute-start | bytes 196616 | tf_op jit(solution)/shard_map/ppermute | solution.py:206
  17.6 5.6 %collective-permute-start.3 = (bf16[4,64,128]{2,1,0:T(8,128)(2,1)S(1)}, bf16[4,64,128]{2,1,0:T(8,128)(2,1)S(1)}, u32[]{:S(2)}, u32[]{:S(2)}) collective-permute-start(bf16[4,64,128]{2,1,0:T(8,128)(2,1)S(1)} %get-tuple-element.13), channel_id=1, source_target_pairs={{1,2},{3,4},{5,6},{2,1},{4,3},{6,5},{9,10},{11,12},{13,14},{10,9},... | collective-permute-start | bytes 196616 | tf_op jit(solution)/shard_map/ppermute | solution.py:206

commit v3 on v2

--- a/solution.py
+++ b/solution.py
@@ -28,7 +28,7 @@
 PARAMS = pltpu.CompilerParams(vmem_limit_bytes=16 << 20)
 
 
-def pack_kernel(fx_ref, fy_ref, disp_ref, adj_ref, ul_ref, x1_ref, x2_ref, y1_ref, y2_ref, disp, adj, fx, fy, sems):
+def pack_kernel(fx_ref, fy_ref, disp_ref, adj_ref, ul_ref, x2_ref, x1_ref, y2_ref, y1_ref, disp, adj, fx, fy, sems):
     pairs = ((disp_ref, disp), (adj_ref, adj), (fx_ref, fx), (fy_ref, fy))
     copies = [pltpu.make_async_copy(src, dst, sems.at[i]) for i, (src, dst) in enumerate(pairs)]
     for copy in copies:
@@ -89,7 +89,7 @@
 
 
 def element_kernel(rows_ref, cols_ref, density_ref, weight_ref, owner_ref, region_ref, k_ref, ul_ref,
-                   x1_ref, x2_ref, y1_ref, y2_ref, sent_ref, ext, same8, cross8):
+                   x2_ref, x1_ref, y2_ref, y1_ref, sent_ref, ext, same8, cross8):
     odd_x = lax.rem(lax.axis_index("z"), 2)
     odd_y = lax.axis_index("c")
     ext[:NB] = ul_ref[...]
@@ -141,7 +141,7 @@
         sent_ref[o, NREG:, :] = jnp.where(place == 0, totals, jnp.where(place == 1, energy_total, 0.0))
 
 
-def elements(rows, cols, density, weight, owner, region, k, ul, x1, x2, y1, y2):
+def elements(rows, cols, density, weight, owner, region, k, ul, x2, x1, y2, y1):
     return pl.pallas_call(
         element_kernel,
         out_shape=jax.ShapeDtypeStruct((OWNERS, SENT_ROWS, LANES), F32),
@@ -150,7 +150,7 @@
         scratch_shapes=[pltpu.VMEM((NT, BS, LANES), BF16), pltpu.VMEM((NT * 8, LANES), F32), pltpu.VMEM((NT * 8, LANES), F32)],
         compiler_params=PARAMS,
     )(rows, cols, density.reshape(1, NT), weight.reshape(1, NT), owner.reshape(1, NT), region.reshape(1, NT),
-      k, ul, x1, x2, y1, y2)
+      k, ul, x2, x1, y2, y1)
 
 
 def region_kernel(got_ref, out_ref, energy_ref):
@@ -190,7 +190,7 @@
 
 
 def swaps(axes, size):
-    for start in (0, 1):
+    for start in (1, 0):
         firsts = range(start, size - 1, 2)
         yield axes, [(i, i + 1) for i in firsts] + [(i + 1, i) for i in firsts]
 

time: 66.6 us -> 65 us (0.976)
  waiting for transfers between devices: 3.06 us -> 0.29 us
  blocking collectives: 39.5 us -> 41.9 us
  starting transfers between devices: 16.9 us -> 15.7 us
    ppermute x4, waiting for transfers between devices: 3.06 us -> 0.29 us  [shards(): lax.ppermute(face, axes, pairs)]
    all_to_all x2, blocking collectives: 39.5 us -> 41.9 us  [exchange(): return lax.all_to_all(x, axes, split_axis=0, concat_axis=0, tiled=True)]
    ppermute x4, starting transfers between devices: 16.9 us -> 15.7 us  [shards(): lax.ppermute(face, axes, pairs)]
where the time goes in v3:
time: 65 us; the launch traced here: 64.7 us
  blocking collectives  41.9 us (64%)
  starting transfers between devices  15.7 us (24%)
  Pallas kernels  5.99 us (9%)
  between operations  0.81 us (1%)
    all_to_all x2, blocking collectives, exchange(): return lax.all_to_all(x, axes, split_axis=0, concat_axis=0, tiled=True)  41.9 us
    ppermute x4, starting transfers between devices, shards(): lax.ppermute(face, axes, pairs)  15.7 us
    pallas_call x1, Pallas kernels, elements(): pl.pallas_call(element_kernel, out_shape=jax.ShapeDtypeStruct((OWNERS, SE...  2.23 us
    pallas_call x1, Pallas kernels, pack(): pl.pallas_call(pack_kernel, out_shape=[jax.ShapeDtypeStruct((n, BS, LANES...  1.87 us
  transfers between devices with their start and end apart: 4, of which 1 were waited for; matrix products, arithmetic and copies ran while one was open for 0% of the time, Pallas kernels for 1%

profile of v3, /device:TPU:1, one launch (start us, length us, event | category | flops | bytes accessed | tf_op | source)
XLA Modules:
  0.0 64.7 jit_solution(10634132143632386931)
XLA Ops:
  0.6 0.0 copy-start
  0.6 0.0 copy-start.3
  0.7 0.0 copy-start.4
  0.7 0.0 copy-start.5
  0.7 0.0 copy-start.6
  0.7 0.0 copy-start.1
  0.7 0.0 copy-start.2
  0.7 1.9 %shard_map.123 = (bf16[64,64,128]{2,1,0:T(8,128)(2,1)S(1)}, bf16[12,64,128]{2,1,0:T(8,128)(2,1)S(1)}, bf16[12,64,128]{2,1,0:T(8,128)(2,1)S(1)}, bf16[4,64,128]{2,1,0:T(8,128)(2,1)S(1)}, bf16[4,64,128]{2,1,0:T(8,128)(2,1)S(1)}) custom-call(s32[1,2,12]{2,1,0:T(2,128)} %fx_ref.1, s32[1,2,4]{2,1,0:T(2,128)} %fy_ref.1, bf16[64,4096]{1,0:T(8,128)(2,1)} %disp_ref.1, ...), custom_call_target="tpu_custom_call" | custom-call | tf_op jit(solution)/shard_map/pallas_call | solution.py:52
  2.6 0.7 %collective-permute-start = (bf16[12,64,128]{2,1,0:T(8,128)(2,1)S(1)}, bf16[12,64,128]{2,1,0:T(8,128)(2,1)S(1)}, u32[]{:S(2)}, u32[]{:S(2)}) collective-permute-start(bf16[12,64,128]{2,1,0:T(8,128)(2,1)S(1)} %get-tuple-element.10), channel_id=1, source_target_pairs={{8,16},{24,32},{40,48},{56,64},{72,80},{88,96},{104,112},{120,128}... | collective-permute-start | bytes 589832 | tf_op jit(solution)/shard_map/ppermute | solution.py:206
  3.3 8.2 %collective-permute-start.1 = (bf16[12,64,128]{2,1,0:T(8,128)(2,1)S(1)}, bf16[12,64,128]{2,1,0:T(8,128)(2,1)S(1)}, u32[]{:S(2)}, u32[]{:S(2)}) collective-permute-start(bf16[12,64,128]{2,1,0:T(8,128)(2,1)S(1)} %get-tuple-element.11), channel_id=1, source_target_pairs={{0,8},{16,24},{32,40},{48,56},{64,72},{80,88},{96,104},{112,120},{... | collective-permute-start | bytes 589832 | tf_op jit(solution)/shard_map/ppermute | solution.py:206
  11.4 4.2 %collective-permute-start.2 = (bf16[4,64,128]{2,1,0:T(8,128)(2,1)S(1)}, bf16[4,64,128]{2,1,0:T(8,128)(2,1)S(1)}, u32[]{:S(2)}, u32[]{:S(2)}) collective-permute-start(bf16[4,64,128]{2,1,0:T(8,128)(2,1)S(1)} %get-tuple-element.12), channel_id=1, source_target_pairs={{1,2},{3,4},{5,6},{2,1},{4,3},{6,5},{9,10},{11,12},{13,14},{10,9},... | collective-permute-start | bytes 196616 | tf_op jit(solution)/shard_map/ppermute | solution.py:206
  15.7 2.6 %collective-permute-start.3 = (bf16[4,64,128]{2,1,0:T(8,128)(2,1)S(1)}, bf16[4,64,128]{2,1,0:T(8,128)(2,1)S(1)}, u32[]{:S(2)}, u32[]{:S(2)}) collective-permute-start(bf16[4,64,128]{2,1,0:T(8,128)(2,1)S(1)} %get-tuple-element.13), channel_id=1, source_target_pairs={{0,1},{2,3},{4,5},{6,7},{1,0},{3,2},{5,4},{7,6},{8,9},{10,11},{12,... | collective-permute-start | bytes 196616 | tf_op jit(solution)/shard_map/ppermute | solution.py:206
  18.3 0.0 copy-done
  18.3 0.6 shard_map.122.k_ref
  18.9 0.0 collective-permute-done.2.y2_ref
  18.9 0.3 collective-permute-done.3.y1_ref
  19.2 0.0 collective-permute-done.x2_ref
  19.2 0.0 collective-permute-done.1.x1_ref
  19.2 0.0 copy-done.3
  19.2 0.0 copy-done.4
  19.2 0.0 copy-done.5
  19.2 0.0 copy-done.6
  19.2 0.0 copy-done.1
  19.2 0.0 copy-done.2
  19.2 2.2 %shard_map.124 = f32[8,40,128]{2,1,0:T(8,128)S(1)} custom-call(s32[96]{0:T(128)S(1)} %copy-done.1, s32[96]{0:T(128)S(1)} %copy-done.2, f32[1,96]{1,0:T(1,128)S(1)} %bitcast.4, f32[1,96]{1,0:T(1,128)S(1)} %bitcast.5, s32[1,96]{1,0:T(1,128)S(1)} %bitcast.6, s32[1,96]{1,0:T(1,128)S(1)} %bitcast.7, bf16[96,64,128]{2,1,0:T(8,128)(2,1)S(1)} %shard_map.122.k_ref, ...), custom_call_target="tpu_custom_call" | custom-call | tf_op jit(solution)/shard_map/pallas_call | solution.py:145
  21.5 10.1 %all_to_all.10.got_ref = f32[8,40,128]{2,1,0:T(8,128)S(1)} all-to-all(f32[8,40,128]{2,1,0:T(8,128)S(1)} %shard_map.124), channel_id=1, replica_groups=mesh['y'=8,'z'=12,'x'=4,'c'=2] {'x','c'}, dimensions={0} | all-to-all | bytes 327680 | tf_op jit(solution)/shard_map/all_to_all | solution.py:199
  31.6 0.7 %shard_map.125 = (f32[32,128]{1,0:T(8,128)}, f32[96,1,128]{2,1,0:T(1,128)S(1)}) custom-call(f32[8,40,128]{2,1,0:T(8,128)S(1)} %all_to_all.10.got_ref), custom_call_target="tpu_custom_call" | custom-call | tf_op jit(solution)/shard_map/pallas_call | solution.py:169
  32.3 31.8 %all_to_all.11.got_ref = f32[96,1,128]{2,1,0:T(1,128)S(1)} all-to-all(f32[96,1,128]{2,1,0:T(1,128)S(1)} %get-tuple-element.15), channel_id=1, replica_groups=mesh['y'=8,'z'=12,'x'=4,'c'=2] {'y','z'}, dimensions={0} | all-to-all | bytes 98304 | tf_op jit(solution)/shard_map/all_to_all | solution.py:199
  64.1 0.6 shard_map.126
Async XLA Ops:
  0.6 17.7 %copy-start = (bf16[96,4096]{1,0:T(8,128)(2,1)S(1)}, bf16[96,4096]{1,0:T(8,128)(2,1)}, u32[]{:S(2)}) copy-start(bf16[96,4096]{1,0:T(8,128)(2,1)} %tiles_ref.1) | copy-start | bytes 2359300
  0.6 18.5 %copy-start.3 = (f32[96]{0:T(128)S(1)}, f32[96]{0:T(128)}, u32[]{:S(2)}) copy-start(f32[96]{0:T(128)} %param.16) | copy-start | bytes 1156
  0.7 18.5 %copy-start.4 = (f32[96]{0:T(128)S(1)}, f32[96]{0:T(128)}, u32[]{:S(2)}) copy-start(f32[96]{0:T(128)} %param.17) | copy-start | bytes 1156
  0.7 18.5 %copy-start.5 = (s32[96,1]{0,1:T(1,128)S(1)}, s32[96,1]{0,1:T(1,128)}, u32[]{:S(2)}) copy-start(s32[96,1]{0,1:T(1,128)} %param.18) | copy-start | bytes 1156
  0.7 18.5 %copy-start.6 = (s32[96]{0:T(128)S(1)}, s32[96]{0:T(128)}, u32[]{:S(2)}) copy-start(s32[96]{0:T(128)} %param.19) | copy-start | bytes 1156
  0.7 18.5 %copy-start.1 = (s32[96]{0:T(128)S(1)}, s32[96]{0:T(128)}, u32[]{:S(2)}) copy-start(s32[96]{0:T(128)} %rows_ref.1) | copy-start | bytes 1156
  0.7 18.5 %copy-start.2 = (s32[96]{0:T(128)S(1)}, s32[96]{0:T(128)}, u32[]{:S(2)}) copy-start(s32[96]{0:T(128)} %cols_ref.1) | copy-start | bytes 1156
  2.6 16.6 %collective-permute-start = (bf16[12,64,128]{2,1,0:T(8,128)(2,1)S(1)}, bf16[12,64,128]{2,1,0:T(8,128)(2,1)S(1)}, u32[]{:S(2)}, u32[]{:S(2)}) collective-permute-start(bf16[12,64,128]{2,1,0:T(8,128)(2,1)S(1)} %get-tuple-element.10), channel_id=1, source_target_pairs={{8,16},{24,32},{40,48},{56,64},{72,80},{88,96},{104,112},{120,128}... | collective-permute-start | bytes 589832 | tf_op jit(solution)/shard_map/ppermute | solution.py:206
  3.3 15.9 %collective-permute-start.1 = (bf16[12,64,128]{2,1,0:T(8,128)(2,1)S(1)}, bf16[12,64,128]{2,1,0:T(8,128)(2,1)S(1)}, u32[]{:S(2)}, u32[]{:S(2)}) collective-permute-start(bf16[12,64,128]{2,1,0:T(8,128)(2,1)S(1)} %get-tuple-element.11), channel_id=1, source_target_pairs={{0,8},{16,24},{32,40},{48,56},{64,72},{80,88},{96,104},{112,120},{... | collective-permute-start | bytes 589832 | tf_op jit(solution)/shard_map/ppermute | solution.py:206
  11.4 7.5 %collective-permute-start.2 = (bf16[4,64,128]{2,1,0:T(8,128)(2,1)S(1)}, bf16[4,64,128]{2,1,0:T(8,128)(2,1)S(1)}, u32[]{:S(2)}, u32[]{:S(2)}) collective-permute-start(bf16[4,64,128]{2,1,0:T(8,128)(2,1)S(1)} %get-tuple-element.12), channel_id=1, source_target_pairs={{1,2},{3,4},{5,6},{2,1},{4,3},{6,5},{9,10},{11,12},{13,14},{10,9},... | collective-permute-start | bytes 196616 | tf_op jit(solution)/shard_map/ppermute | solution.py:206
  15.7 3.5 %collective-permute-start.3 = (bf16[4,64,128]{2,1,0:T(8,128)(2,1)S(1)}, bf16[4,64,128]{2,1,0:T(8,128)(2,1)S(1)}, u32[]{:S(2)}, u32[]{:S(2)}) collective-permute-start(bf16[4,64,128]{2,1,0:T(8,128)(2,1)S(1)} %get-tuple-element.13), channel_id=1, source_target_pairs={{0,1},{2,3},{4,5},{6,7},{1,0},{3,2},{5,4},{7,6},{8,9},{10,11},{12,... | collective-permute-start | bytes 196616 | tf_op jit(solution)/shard_map/ppermute | solution.py:206

commit v4 on v3

--- a/solution.py
+++ b/solution.py
@@ -22,23 +22,28 @@
 GROUP = 32
 F32 = jnp.float32
 BF16 = jnp.bfloat16
-SMEM = pl.BlockSpec(memory_space=pltpu.SMEM)
 VMEM = pl.BlockSpec(memory_space=pltpu.VMEM)
 HBM = pl.BlockSpec(memory_space=pltpu.HBM)
 PARAMS = pltpu.CompilerParams(vmem_limit_bytes=16 << 20)
 
 
 def pack_kernel(fx_ref, fy_ref, disp_ref, adj_ref, ul_ref, x2_ref, x1_ref, y2_ref, y1_ref, disp, adj, fx, fy, sems):
-    pairs = ((disp_ref, disp), (adj_ref, adj), (fx_ref, fx), (fy_ref, fy))
+    half = NB // 2
+    spans = (slice(0, half), slice(half, NB))
+    pairs = [(ref.at[span], buf.at[span]) for span in spans for ref, buf in ((disp_ref, disp), (adj_ref, adj))]
+    pairs += [(fx_ref, fx), (fy_ref, fy)]
     copies = [pltpu.make_async_copy(src, dst, sems.at[i]) for i, (src, dst) in enumerate(pairs)]
     for copy in copies:
         copy.start()
-    for copy in copies:
-        copy.wait()
-    u = disp[...].reshape(NB, HALF, LANES)
-    v = adj[...].reshape(NB, HALF, LANES)
-    ul_ref[:, :HALF, :] = jnp.concatenate([u[..., :R], v[..., :R]], axis=-1)
-    ul_ref[:, HALF:, :] = jnp.concatenate([u[..., R:], v[..., R:]], axis=-1)
+    for i, span in enumerate(spans):
+        copies[2 * i].wait()
+        copies[2 * i + 1].wait()
+        u = disp[span, :].reshape(half, HALF, LANES)
+        v = adj[span, :].reshape(half, HALF, LANES)
+        ul_ref[span, :HALF, :] = jnp.concatenate([u[..., :R], v[..., :R]], axis=-1)
+        ul_ref[span, HALF:, :] = jnp.concatenate([u[..., R:], v[..., R:]], axis=-1)
+    copies[4].wait()
+    copies[5].wait()
     odd_x = lax.rem(lax.axis_index("z"), 2)
     odd_y = lax.axis_index("c")
     for out, idx, side, count in ((x1_ref, fx, odd_x, NIX), (x2_ref, fx, 1 - odd_x, NIX),
@@ -56,7 +61,7 @@
         out_specs=[VMEM] * 5,
         scratch_shapes=[pltpu.VMEM((NB, BS * R), BF16), pltpu.VMEM((NB, BS * R), BF16),
                         pltpu.SMEM((1, 2, NIX), jnp.int32), pltpu.SMEM((1, 2, NIY), jnp.int32),
-                        pltpu.SemaphoreType.DMA((4,))],
+                        pltpu.SemaphoreType.DMA((6,))],
         compiler_params=PARAMS,
     )(*args)
 
@@ -89,7 +94,10 @@
 
 
 def element_kernel(rows_ref, cols_ref, density_ref, weight_ref, owner_ref, region_ref, k_ref, ul_ref,
-                   x2_ref, x1_ref, y2_ref, y1_ref, sent_ref, ext, same8, cross8):
+                   x2_ref, x1_ref, y2_ref, y1_ref, sent_ref, rows, cols, ext, same8, cross8, sems):
+    copies = [pltpu.make_async_copy(src, dst, sems.at[i]) for i, (src, dst) in enumerate(((rows_ref, rows), (cols_ref, cols)))]
+    for copy in copies:
+        copy.start()
     odd_x = lax.rem(lax.axis_index("z"), 2)
     odd_y = lax.axis_index("c")
     ext[:NB] = ul_ref[...]
@@ -97,12 +105,23 @@
     ext[pl.ds(NB + NIX * odd_x, NIX)] = x2_ref[...]
     ext[pl.ds(NB + 2 * NIX + NIY * (1 - odd_y), NIY)] = y1_ref[...]
     ext[pl.ds(NB + 2 * NIX + NIY * odd_y, NIY)] = y2_ref[...]
+    weight = column(weight_ref[...])
+    ident = owner_ref[...] * NREG + region_ref[...]
+    ident_column = column(ident.astype(F32)).astype(jnp.int32)
+    lane = lax.broadcasted_iota(jnp.int32, (NT, LANES), 1)
+    place = lax.broadcasted_iota(jnp.int32, (8, LANES), 0)
+    for o in range(OWNERS):
+        hit = (ident_column == lane + o * NREG) & (lane < NREG)
+        totals = jnp.sum(jnp.where(hit, weight, 0.0), axis=0, keepdims=True)
+        sent_ref[o, NREG:, :] = jnp.where(place == 0, totals, 0.0)
+    for copy in copies:
+        copy.wait()
 
     def body(g, carry):
         for i in range(GROUP):
             t = g * GROUP + i
-            row = ul_ref[rows_ref[t]].astype(F32)
-            prod = jnp.dot(k_ref[t][:, :BS], ext[cols_ref[t]], preferred_element_type=F32)
+            row = ul_ref[rows[t]].astype(F32)
+            prod = jnp.dot(k_ref[t][:, :BS], ext[cols[t]], preferred_element_type=F32)
             at = pl.ds(pl.multiple_of(t * 8, 8), 8)
             same8[at, :] = jnp.sum((row * prod).reshape(8, 8, LANES), axis=0)
             cross8[at, :] = jnp.sum((pltpu.roll(row, R, 1) * prod).reshape(8, 8, LANES), axis=0)
@@ -118,11 +137,9 @@
     cross = cross + pltpu.roll(cross, R, 1)
     energy_total = jnp.sum(energy, axis=0, keepdims=True)
     rho = column(density_ref[...])
-    weight = column(weight_ref[...])
     sens = -(3.0 * rho * rho / (2.0 * math.sqrt(BS))) * cross
     left = lax.broadcasted_iota(jnp.int32, (NT, LANES), 1) < R
     payload = weight * jnp.where(left, sens, pltpu.roll(energy, R, 1))
-    ident = owner_ref[...] * NREG + region_ref[...]
     onehot = (lax.broadcasted_iota(jnp.int32, (OWNERS * NREG, NT), 0) == ident).astype(F32).astype(BF16)
     high = payload.astype(BF16)
     rest = payload - high.astype(F32)
@@ -131,23 +148,19 @@
     sums = (jnp.dot(onehot, high, preferred_element_type=F32)
             + jnp.dot(onehot, mid, preferred_element_type=F32)
             + jnp.dot(onehot, low, preferred_element_type=F32))
-    ident_column = column(ident.astype(F32)).astype(jnp.int32)
-    lane = lax.broadcasted_iota(jnp.int32, (NT, LANES), 1)
-    place = lax.broadcasted_iota(jnp.int32, (8, LANES), 0)
     for o in range(OWNERS):
         sent_ref[o, :NREG, :] = sums[o * NREG:(o + 1) * NREG, :]
-        hit = (ident_column == lane + o * NREG) & (lane < NREG)
-        totals = jnp.sum(jnp.where(hit, weight, 0.0), axis=0, keepdims=True)
-        sent_ref[o, NREG:, :] = jnp.where(place == 0, totals, jnp.where(place == 1, energy_total, 0.0))
+        sent_ref[o, NREG + 1:NREG + 2, :] = energy_total
 
 
 def elements(rows, cols, density, weight, owner, region, k, ul, x2, x1, y2, y1):
     return pl.pallas_call(
         element_kernel,
         out_shape=jax.ShapeDtypeStruct((OWNERS, SENT_ROWS, LANES), F32),
-        in_specs=[SMEM, SMEM] + [VMEM] * 10,
+        in_specs=[VMEM] * 12,
         out_specs=VMEM,
-        scratch_shapes=[pltpu.VMEM((NT, BS, LANES), BF16), pltpu.VMEM((NT * 8, LANES), F32), pltpu.VMEM((NT * 8, LANES), F32)],
+        scratch_shapes=[pltpu.SMEM((NT,), jnp.int32), pltpu.SMEM((NT,), jnp.int32), pltpu.VMEM((NT, BS, LANES), BF16),
+                        pltpu.VMEM((NT * 8, LANES), F32), pltpu.VMEM((NT * 8, LANES), F32), pltpu.SemaphoreType.DMA((2,))],
         compiler_params=PARAMS,
     )(rows, cols, density.reshape(1, NT), weight.reshape(1, NT), owner.reshape(1, NT), region.reshape(1, NT),
       k, ul, x2, x1, y2, y1)

time: 65 us -> 64.8 us (level)
  no operation moved by 1% of the time
where the time goes in v4:
time: 64.8 us; the launch traced here: 64.5 us
  blocking collectives  41.9 us (65%)
  starting transfers between devices  15.7 us (24%)
  Pallas kernels  5.78 us (9%)
  between operations  0.81 us (1%)
    all_to_all x2, blocking collectives, exchange(): return lax.all_to_all(x, axes, split_axis=0, concat_axis=0, tiled=True)  41.9 us
    ppermute x4, starting transfers between devices, shards(): lax.ppermute(face, axes, pairs)  15.7 us
    pallas_call x1, Pallas kernels, elements(): pl.pallas_call(element_kernel, out_shape=jax.ShapeDtypeStruct((OWNERS, SE...  2.11 us
    pallas_call x1, Pallas kernels, pack(): pl.pallas_call(pack_kernel, out_shape=[jax.ShapeDtypeStruct((n, BS, LANES...  1.79 us
  transfers between devices with their start and end apart: 4, of which 1 were waited for; matrix products, arithmetic and copies ran while one was open for 0% of the time, Pallas kernels for 1%

profile of v4, /device:TPU:1, one launch (start us, length us, event | category | flops | bytes accessed | tf_op | source)
XLA Modules:
  0.0 64.5 jit_solution(7705453481068435039)
XLA Ops:
  0.6 0.0 copy-start
  0.6 0.0 copy-start.3
  0.7 0.0 copy-start.4
  0.7 0.0 copy-start.5
  0.7 0.0 copy-start.6
  0.7 0.0 copy-start.1
  0.7 0.0 copy-start.2
  0.7 1.8 %shard_map.123 = (bf16[64,64,128]{2,1,0:T(8,128)(2,1)S(1)}, bf16[12,64,128]{2,1,0:T(8,128)(2,1)S(1)}, bf16[12,64,128]{2,1,0:T(8,128)(2,1)S(1)}, bf16[4,64,128]{2,1,0:T(8,128)(2,1)S(1)}, bf16[4,64,128]{2,1,0:T(8,128)(2,1)S(1)}) custom-call(s32[1,2,12]{2,1,0:T(2,128)} %fx_ref.1, s32[1,2,4]{2,1,0:T(2,128)} %fy_ref.1, bf16[64,4096]{1,0:T(8,128)(2,1)} %disp_ref.1, ...), custom_call_target="tpu_custom_call" | custom-call | tf_op jit(solution)/shard_map/pallas_call | solution.py:57
  2.5 0.7 %collective-permute-start = (bf16[12,64,128]{2,1,0:T(8,128)(2,1)S(1)}, bf16[12,64,128]{2,1,0:T(8,128)(2,1)S(1)}, u32[]{:S(2)}, u32[]{:S(2)}) collective-permute-start(bf16[12,64,128]{2,1,0:T(8,128)(2,1)S(1)} %get-tuple-element.10), channel_id=1, source_target_pairs={{8,16},{24,32},{40,48},{56,64},{72,80},{88,96},{104,112},{120,128}... | collective-permute-start | bytes 589832 | tf_op jit(solution)/shard_map/ppermute | solution.py:219
  3.2 8.2 %collective-permute-start.1 = (bf16[12,64,128]{2,1,0:T(8,128)(2,1)S(1)}, bf16[12,64,128]{2,1,0:T(8,128)(2,1)S(1)}, u32[]{:S(2)}, u32[]{:S(2)}) collective-permute-start(bf16[12,64,128]{2,1,0:T(8,128)(2,1)S(1)} %get-tuple-element.11), channel_id=1, source_target_pairs={{0,8},{16,24},{32,40},{48,56},{64,72},{80,88},{96,104},{112,120},{... | collective-permute-start | bytes 589832 | tf_op jit(solution)/shard_map/ppermute | solution.py:219
  11.3 4.2 %collective-permute-start.2 = (bf16[4,64,128]{2,1,0:T(8,128)(2,1)S(1)}, bf16[4,64,128]{2,1,0:T(8,128)(2,1)S(1)}, u32[]{:S(2)}, u32[]{:S(2)}) collective-permute-start(bf16[4,64,128]{2,1,0:T(8,128)(2,1)S(1)} %get-tuple-element.12), channel_id=1, source_target_pairs={{1,2},{3,4},{5,6},{2,1},{4,3},{6,5},{9,10},{11,12},{13,14},{10,9},... | collective-permute-start | bytes 196616 | tf_op jit(solution)/shard_map/ppermute | solution.py:219
  15.6 2.6 %collective-permute-start.3 = (bf16[4,64,128]{2,1,0:T(8,128)(2,1)S(1)}, bf16[4,64,128]{2,1,0:T(8,128)(2,1)S(1)}, u32[]{:S(2)}, u32[]{:S(2)}) collective-permute-start(bf16[4,64,128]{2,1,0:T(8,128)(2,1)S(1)} %get-tuple-element.13), channel_id=1, source_target_pairs={{0,1},{2,3},{4,5},{6,7},{1,0},{3,2},{5,4},{7,6},{8,9},{10,11},{12,... | collective-permute-start | bytes 196616 | tf_op jit(solution)/shard_map/ppermute | solution.py:219
  18.2 0.0 copy-done
  18.2 0.6 shard_map.122.k_ref
  18.8 0.0 collective-permute-done.2.y2_ref
  18.8 0.3 collective-permute-done.3.y1_ref
  19.1 0.0 collective-permute-done.x2_ref
  19.1 0.0 collective-permute-done.1.x1_ref
  19.1 0.0 copy-done.3
  19.1 0.0 copy-done.4
  19.1 0.0 copy-done.5
  19.1 0.0 copy-done.6
  19.1 0.0 copy-done.1
  19.1 0.0 copy-done.2
  19.2 2.1 %shard_map.124 = f32[8,40,128]{2,1,0:T(8,128)S(1)} custom-call(s32[96]{0:T(128)S(1)} %copy-done.1, s32[96]{0:T(128)S(1)} %copy-done.2, f32[1,96]{1,0:T(1,128)S(1)} %bitcast.4, f32[1,96]{1,0:T(1,128)S(1)} %bitcast.5, s32[1,96]{1,0:T(1,128)S(1)} %bitcast.6, s32[1,96]{1,0:T(1,128)S(1)} %bitcast.7, bf16[96,64,128]{2,1,0:T(8,128)(2,1)S(1)} %shard_map.122.k_ref, ...), custom_call_target="tpu_custom_call" | custom-call | tf_op jit(solution)/shard_map/pallas_call | solution.py:157
  21.3 10.1 %all_to_all.10.got_ref = f32[8,40,128]{2,1,0:T(8,128)S(1)} all-to-all(f32[8,40,128]{2,1,0:T(8,128)S(1)} %shard_map.124), channel_id=1, replica_groups=mesh['y'=8,'z'=12,'x'=4,'c'=2] {'x','c'}, dimensions={0} | all-to-all | bytes 327680 | tf_op jit(solution)/shard_map/all_to_all | solution.py:212
  31.4 0.7 %shard_map.125 = (f32[32,128]{1,0:T(8,128)}, f32[96,1,128]{2,1,0:T(1,128)S(1)}) custom-call(f32[8,40,128]{2,1,0:T(8,128)S(1)} %all_to_all.10.got_ref), custom_call_target="tpu_custom_call" | custom-call | tf_op jit(solution)/shard_map/pallas_call | solution.py:182
  32.1 31.8 %all_to_all.11.got_ref = f32[96,1,128]{2,1,0:T(1,128)S(1)} all-to-all(f32[96,1,128]{2,1,0:T(1,128)S(1)} %get-tuple-element.15), channel_id=1, replica_groups=mesh['y'=8,'z'=12,'x'=4,'c'=2] {'y','z'}, dimensions={0} | all-to-all | bytes 98304 | tf_op jit(solution)/shard_map/all_to_all | solution.py:212
  63.9 0.6 shard_map.126
Async XLA Ops:
  0.6 17.6 %copy-start = (bf16[96,4096]{1,0:T(8,128)(2,1)S(1)}, bf16[96,4096]{1,0:T(8,128)(2,1)}, u32[]{:S(2)}) copy-start(bf16[96,4096]{1,0:T(8,128)(2,1)} %tiles_ref.1) | copy-start | bytes 2359300
  0.6 18.5 %copy-start.3 = (f32[96]{0:T(128)S(1)}, f32[96]{0:T(128)}, u32[]{:S(2)}) copy-start(f32[96]{0:T(128)} %param.16) | copy-start | bytes 1156
  0.7 18.5 %copy-start.4 = (f32[96]{0:T(128)S(1)}, f32[96]{0:T(128)}, u32[]{:S(2)}) copy-start(f32[96]{0:T(128)} %param.17) | copy-start | bytes 1156
  0.7 18.5 %copy-start.5 = (s32[96,1]{0,1:T(1,128)S(1)}, s32[96,1]{0,1:T(1,128)}, u32[]{:S(2)}) copy-start(s32[96,1]{0,1:T(1,128)} %param.18) | copy-start | bytes 1156
  0.7 18.5 %copy-start.6 = (s32[96]{0:T(128)S(1)}, s32[96]{0:T(128)}, u32[]{:S(2)}) copy-start(s32[96]{0:T(128)} %param.19) | copy-start | bytes 1156
  0.7 18.5 %copy-start.1 = (s32[96]{0:T(128)S(1)}, s32[96]{0:T(128)}, u32[]{:S(2)}) copy-start(s32[96]{0:T(128)} %rows_ref.1) | copy-start | bytes 1156
  0.7 18.5 %copy-start.2 = (s32[96]{0:T(128)S(1)}, s32[96]{0:T(128)}, u32[]{:S(2)}) copy-start(s32[96]{0:T(128)} %cols_ref.1) | copy-start | bytes 1156
  2.5 16.6 %collective-permute-start = (bf16[12,64,128]{2,1,0:T(8,128)(2,1)S(1)}, bf16[12,64,128]{2,1,0:T(8,128)(2,1)S(1)}, u32[]{:S(2)}, u32[]{:S(2)}) collective-permute-start(bf16[12,64,128]{2,1,0:T(8,128)(2,1)S(1)} %get-tuple-element.10), channel_id=1, source_target_pairs={{8,16},{24,32},{40,48},{56,64},{72,80},{88,96},{104,112},{120,128}... | collective-permute-start | bytes 589832 | tf_op jit(solution)/shard_map/ppermute | solution.py:219
  3.2 15.9 %collective-permute-start.1 = (bf16[12,64,128]{2,1,0:T(8,128)(2,1)S(1)}, bf16[12,64,128]{2,1,0:T(8,128)(2,1)S(1)}, u32[]{:S(2)}, u32[]{:S(2)}) collective-permute-start(bf16[12,64,128]{2,1,0:T(8,128)(2,1)S(1)} %get-tuple-element.11), channel_id=1, source_target_pairs={{0,8},{16,24},{32,40},{48,56},{64,72},{80,88},{96,104},{112,120},{... | collective-permute-start | bytes 589832 | tf_op jit(solution)/shard_map/ppermute | solution.py:219
  11.3 7.5 %collective-permute-start.2 = (bf16[4,64,128]{2,1,0:T(8,128)(2,1)S(1)}, bf16[4,64,128]{2,1,0:T(8,128)(2,1)S(1)}, u32[]{:S(2)}, u32[]{:S(2)}) collective-permute-start(bf16[4,64,128]{2,1,0:T(8,128)(2,1)S(1)} %get-tuple-element.12), channel_id=1, source_target_pairs={{1,2},{3,4},{5,6},{2,1},{4,3},{6,5},{9,10},{11,12},{13,14},{10,9},... | collective-permute-start | bytes 196616 | tf_op jit(solution)/shard_map/ppermute | solution.py:219
  15.6 3.5 %collective-permute-start.3 = (bf16[4,64,128]{2,1,0:T(8,128)(2,1)S(1)}, bf16[4,64,128]{2,1,0:T(8,128)(2,1)S(1)}, u32[]{:S(2)}, u32[]{:S(2)}) collective-permute-start(bf16[4,64,128]{2,1,0:T(8,128)(2,1)S(1)} %get-tuple-element.13), channel_id=1, source_target_pairs={{0,1},{2,3},{4,5},{6,7},{1,0},{3,2},{5,4},{7,6},{8,9},{10,11},{12,... | collective-permute-start | bytes 196616 | tf_op jit(solution)/shard_map/ppermute | solution.py:219

commit v5 on v4

--- a/solution.py
+++ b/solution.py
@@ -19,7 +19,7 @@
 LANES = 128
 HALF = BS // 2
 SENT_ROWS = 40
-GROUP = 32
+GROUP = 48
 F32 = jnp.float32
 BF16 = jnp.bfloat16
 VMEM = pl.BlockSpec(memory_space=pltpu.VMEM)
@@ -27,11 +27,13 @@
 PARAMS = pltpu.CompilerParams(vmem_limit_bytes=16 << 20)
 
 
-def pack_kernel(fx_ref, fy_ref, disp_ref, adj_ref, ul_ref, x2_ref, x1_ref, y2_ref, y1_ref, disp, adj, fx, fy, sems):
+def pack_kernel(fx_ref, fy_ref, disp_ref, adj_ref, density_ref, weight_ref, owner_ref, region_ref,
+                ul_ref, x2_ref, x1_ref, y2_ref, y1_ref, density, weight, owner, region, disp, adj, fx, fy, sems):
     half = NB // 2
     spans = (slice(0, half), slice(half, NB))
     pairs = [(ref.at[span], buf.at[span]) for span in spans for ref, buf in ((disp_ref, disp), (adj_ref, adj))]
     pairs += [(fx_ref, fx), (fy_ref, fy)]
+    pairs += [(density_ref, density), (weight_ref, weight), (owner_ref, owner), (region_ref, region)]
     copies = [pltpu.make_async_copy(src, dst, sems.at[i]) for i, (src, dst) in enumerate(pairs)]
     for copy in copies:
         copy.start()
@@ -50,23 +52,30 @@
                                   (y1_ref, fy, odd_y, NIY), (y2_ref, fy, 1 - odd_y, NIY)):
         for i in range(count):
             out[i] = ul_ref[idx[0, side, i]]
-
-
-def pack(face_x, face_y, disp, adjoint):
-    args = [pltpu.with_memory_space_constraint(a, pltpu.HBM) for a in (face_x, face_y, disp, adjoint)]
+    for copy in copies[6:]:
+        copy.wait()
+
+
+def pack(*args):
+    args = [pltpu.with_memory_space_constraint(a, pltpu.HBM) for a in args]
     return pl.pallas_call(
         pack_kernel,
-        out_shape=[jax.ShapeDtypeStruct((n, BS, LANES), BF16) for n in (NB, NIX, NIX, NIY, NIY)],
-        in_specs=[HBM] * 4,
-        out_specs=[VMEM] * 5,
+        out_shape=[jax.ShapeDtypeStruct((n, BS, LANES), BF16) for n in (NB, NIX, NIX, NIY, NIY)]
+        + [jax.ShapeDtypeStruct((1, NT), kind) for kind in (F32, F32, jnp.int32, jnp.int32)],
+        in_specs=[HBM] * 8,
+        out_specs=[VMEM] * 9,
         scratch_shapes=[pltpu.VMEM((NB, BS * R), BF16), pltpu.VMEM((NB, BS * R), BF16),
                         pltpu.SMEM((1, 2, NIX), jnp.int32), pltpu.SMEM((1, 2, NIY), jnp.int32),
-                        pltpu.SemaphoreType.DMA((6,))],
+                        pltpu.SemaphoreType.DMA((10,))],
         compiler_params=PARAMS,
     )(*args)
 
 
-def stiffness_kernel(tiles_ref, k_ref):
+def column(row):
+    return jnp.broadcast_to(row, (LANES, NT)).T
+
+
+def stiffness_kernel(density_ref, weight_ref, owner_ref, region_ref, tiles_ref, k_ref, factor_ref, wide_ref, totals_ref):
     pairs = tiles_ref[...].reshape(NT * HALF, LANES)
     source = lax.broadcasted_iota(jnp.int32, (LANES, 2 * LANES), 0)
     target = lax.broadcasted_iota(jnp.int32, (LANES, 2 * LANES), 1)
@@ -76,24 +85,32 @@
     moved = jnp.dot(pairs, order, preferred_element_type=F32).astype(BF16)
     k_ref[:, :HALF, :] = moved[:, :LANES].reshape(NT, HALF, LANES)
     k_ref[:, HALF:, :] = moved[:, LANES:].reshape(NT, HALF, LANES)
-
-
-def stiffness(tiles):
+    rho = column(density_ref[...])
+    factor_ref[...] = -(3.0 * rho * rho / (2.0 * math.sqrt(BS)))
+    weight = column(weight_ref[...])
+    wide_ref[...] = weight
+    ident = column((owner_ref[...] * NREG + region_ref[...]).astype(F32)).astype(jnp.int32)
+    lane = lax.broadcasted_iota(jnp.int32, (NT, LANES), 1)
+    place = lax.broadcasted_iota(jnp.int32, (8, LANES), 0)
+    for o in range(OWNERS):
+        hit = (ident == lane + o * NREG) & (lane < NREG)
+        totals = jnp.sum(jnp.where(hit, weight, 0.0), axis=0, keepdims=True)
+        totals_ref[o] = jnp.where(place == 0, totals, 0.0)
+
+
+def stiffness(density, weight, owner, region, tiles):
     return pl.pallas_call(
         stiffness_kernel,
-        out_shape=jax.ShapeDtypeStruct((NT, BS, LANES), BF16),
-        in_specs=[VMEM],
-        out_specs=VMEM,
+        out_shape=[jax.ShapeDtypeStruct((NT, BS, LANES), BF16), jax.ShapeDtypeStruct((NT, LANES), F32),
+                   jax.ShapeDtypeStruct((NT, LANES), F32), jax.ShapeDtypeStruct((OWNERS, 8, LANES), F32)],
+        in_specs=[VMEM] * 5,
+        out_specs=[VMEM] * 4,
         compiler_params=PARAMS,
         cost_estimate=pl.CostEstimate(flops=0, bytes_accessed=8 << 20, transcendentals=0),
-    )(tiles)
-
-
-def column(row):
-    return jnp.broadcast_to(row, (LANES, NT)).T
-
-
-def element_kernel(rows_ref, cols_ref, density_ref, weight_ref, owner_ref, region_ref, k_ref, ul_ref,
+    )(density, weight, owner, region, tiles)
+
+
+def element_kernel(rows_ref, cols_ref, owner_ref, region_ref, k_ref, factor_ref, wide_ref, totals_ref, ul_ref,
                    x2_ref, x1_ref, y2_ref, y1_ref, sent_ref, rows, cols, ext, same8, cross8, sems):
     copies = [pltpu.make_async_copy(src, dst, sems.at[i]) for i, (src, dst) in enumerate(((rows_ref, rows), (cols_ref, cols)))]
     for copy in copies:
@@ -105,15 +122,6 @@
     ext[pl.ds(NB + NIX * odd_x, NIX)] = x2_ref[...]
     ext[pl.ds(NB + 2 * NIX + NIY * (1 - odd_y), NIY)] = y1_ref[...]
     ext[pl.ds(NB + 2 * NIX + NIY * odd_y, NIY)] = y2_ref[...]
-    weight = column(weight_ref[...])
-    ident = owner_ref[...] * NREG + region_ref[...]
-    ident_column = column(ident.astype(F32)).astype(jnp.int32)
-    lane = lax.broadcasted_iota(jnp.int32, (NT, LANES), 1)
-    place = lax.broadcasted_iota(jnp.int32, (8, LANES), 0)
-    for o in range(OWNERS):
-        hit = (ident_column == lane + o * NREG) & (lane < NREG)
-        totals = jnp.sum(jnp.where(hit, weight, 0.0), axis=0, keepdims=True)
-        sent_ref[o, NREG:, :] = jnp.where(place == 0, totals, 0.0)
     for copy in copies:
         copy.wait()
 
@@ -136,10 +144,10 @@
     energy = same / math.sqrt(BS)
     cross = cross + pltpu.roll(cross, R, 1)
     energy_total = jnp.sum(energy, axis=0, keepdims=True)
-    rho = column(density_ref[...])
-    sens = -(3.0 * rho * rho / (2.0 * math.sqrt(BS))) * cross
+    sens = factor_ref[...] * cross
     left = lax.broadcasted_iota(jnp.int32, (NT, LANES), 1) < R
-    payload = weight * jnp.where(left, sens, pltpu.roll(energy, R, 1))
+    payload = wide_ref[...] * jnp.where(left, sens, pltpu.roll(energy, R, 1))
+    ident = owner_ref[...] * NREG + region_ref[...]
     onehot = (lax.broadcasted_iota(jnp.int32, (OWNERS * NREG, NT), 0) == ident).astype(F32).astype(BF16)
     high = payload.astype(BF16)
     rest = payload - high.astype(F32)
@@ -148,22 +156,22 @@
     sums = (jnp.dot(onehot, high, preferred_element_type=F32)
             + jnp.dot(onehot, mid, preferred_element_type=F32)
             + jnp.dot(onehot, low, preferred_element_type=F32))
+    place = lax.broadcasted_iota(jnp.int32, (8, LANES), 0)
     for o in range(OWNERS):
         sent_ref[o, :NREG, :] = sums[o * NREG:(o + 1) * NREG, :]
-        sent_ref[o, NREG + 1:NREG + 2, :] = energy_total
-
-
-def elements(rows, cols, density, weight, owner, region, k, ul, x2, x1, y2, y1):
+        sent_ref[o, NREG:, :] = jnp.where(place == 1, energy_total, totals_ref[o])
+
+
+def elements(rows, cols, owner, region, k, factor, wide, totals, ul, x2, x1, y2, y1):
     return pl.pallas_call(
         element_kernel,
         out_shape=jax.ShapeDtypeStruct((OWNERS, SENT_ROWS, LANES), F32),
-        in_specs=[VMEM] * 12,
+        in_specs=[VMEM] * 13,
         out_specs=VMEM,
         scratch_shapes=[pltpu.SMEM((NT,), jnp.int32), pltpu.SMEM((NT,), jnp.int32), pltpu.VMEM((NT, BS, LANES), BF16),
                         pltpu.VMEM((NT * 8, LANES), F32), pltpu.VMEM((NT * 8, LANES), F32), pltpu.SemaphoreType.DMA((2,))],
         compiler_params=PARAMS,
-    )(rows, cols, density.reshape(1, NT), weight.reshape(1, NT), owner.reshape(1, NT), region.reshape(1, NT),
-      k, ul, x2, x1, y2, y1)
+    )(rows, cols, owner, region, k, factor, wide, totals, ul, x2, x1, y2, y1)
 
 
 def region_kernel(got_ref, out_ref, energy_ref):
@@ -214,11 +222,12 @@
 
 def shards(disp, adjoint, tiles, tile_rows, tile_cols, density, filter_weight, owner, region, face_x, face_y):
     ny, nz, nx, nc = (lax.axis_size(a) for a in ("y", "z", "x", "c"))
-    ul, *faces = pack(face_x, face_y, disp, adjoint)
+    scalars = [a.reshape(1, NT) for a in (density, filter_weight, owner, region)]
+    ul, *faces, density, weight, owner, region = pack(face_x, face_y, disp, adjoint, *scalars)
     plans = [*swaps(("y", "z"), ny * nz), *swaps(("x", "c"), nx * nc)]
     halos = [lax.ppermute(face, axes, pairs) for face, (axes, pairs) in zip(faces, plans)]
-    k = stiffness(tiles)
-    sent = elements(tile_rows, tile_cols, density, filter_weight, owner, region, k, ul, *halos)
+    k, factor, wide, totals = stiffness(density, weight, owner, region, tiles)
+    sent = elements(tile_rows, tile_cols, owner, region, k, factor, wide, totals, ul, *halos)
     filtered, energy = regions(exchange(sent, ("x", "c")), ny * nz)
     compliance = last(exchange(energy, ("y", "z")), math.sqrt(NT * ny * nz * nx * nc))
     return (filtered, compliance)

time: 64.8 us -> 64.7 us (level)
  no operation moved by 1% of the time
where the time goes in v5:
time: 64.7 us; the launch traced here: 64.4 us
  blocking collectives  42 us (65%)
  starting transfers between devices  15.7 us (24%)
  Pallas kernels  5.72 us (9%)
  between operations  0.74 us (1%)
    all_to_all x2, blocking collectives, exchange(): return lax.all_to_all(x, axes, split_axis=0, concat_axis=0, tiled=True)  42 us
    ppermute x4, starting transfers between devices, shards(): lax.ppermute(face, axes, pairs)  15.7 us
    pallas_call x1, Pallas kernels, elements(): pl.pallas_call(element_kernel, out_shape=jax.ShapeDtypeStruct((OWNERS, SE...  1.98 us
    pallas_call x1, Pallas kernels, pack(): pl.pallas_call(pack_kernel, out_shape=[jax.ShapeDtypeStruct((n, BS, LANES...  1.84 us
  transfers between devices with their start and end apart: 4, of which 1 were waited for; matrix products, arithmetic and copies ran while one was open for 0% of the time, Pallas kernels for 1%

profile of v5, /device:TPU:1, one launch (start us, length us, event | category | flops | bytes accessed | tf_op | source)
XLA Modules:
  0.0 64.4 jit_solution(5386791685656789749)
XLA Ops:
  0.6 0.0 copy-start
  0.6 0.0 copy-start.2
  0.7 0.0 copy-start.1
  0.7 1.8 %shard_map.122 = (bf16[64,64,128]{2,1,0:T(8,128)(2,1)S(1)}, bf16[12,64,128]{2,1,0:T(8,128)(2,1)S(1)}, bf16[12,64,128]{2,1,0:T(8,128)(2,1)S(1)}, bf16[4,64,128]{2...) custom-call(s32[1,2,12]{2,1,0:T(2,128)} %fx_ref.1, ...), custom_call_target="tpu_custom_call" | custom-call | tf_op jit(solution)/shard_map/pallas_call | solution.py:61
  2.5 0.7 %collective-permute-start = (bf16[12,64,128]{2,1,0:T(8,128)(2,1)S(1)}, bf16[12,64,128]{2,1,0:T(8,128)(2,1)S(1)}, u32[]{:S(2)}, u32[]{:S(2)}) collective-permute-start(bf16[12,64,128]{2,1,0:T(8,128)(2,1)S(1)} %get-tuple-element.26), channel_id=1, source_target_pairs={{8,16},{24,32},{40,48},{56,64},{72,80},{88,96},{104,112},{120,128}... | collective-permute-start | bytes 589832 | tf_op jit(solution)/shard_map/ppermute | solution.py:228
  3.2 8.2 %collective-permute-start.1 = (bf16[12,64,128]{2,1,0:T(8,128)(2,1)S(1)}, bf16[12,64,128]{2,1,0:T(8,128)(2,1)S(1)}, u32[]{:S(2)}, u32[]{:S(2)}) collective-permute-start(bf16[12,64,128]{2,1,0:T(8,128)(2,1)S(1)} %get-tuple-element.27), channel_id=1, source_target_pairs={{0,8},{16,24},{32,40},{48,56},{64,72},{80,88},{96,104},{112,120},{... | collective-permute-start | bytes 589832 | tf_op jit(solution)/shard_map/ppermute | solution.py:228
  11.4 4.2 %collective-permute-start.2 = (bf16[4,64,128]{2,1,0:T(8,128)(2,1)S(1)}, bf16[4,64,128]{2,1,0:T(8,128)(2,1)S(1)}, u32[]{:S(2)}, u32[]{:S(2)}) collective-permute-start(bf16[4,64,128]{2,1,0:T(8,128)(2,1)S(1)} %get-tuple-element.28), channel_id=1, source_target_pairs={{1,2},{3,4},{5,6},{2,1},{4,3},{6,5},{9,10},{11,12},{13,14},{10,9},... | collective-permute-start | bytes 196616 | tf_op jit(solution)/shard_map/ppermute | solution.py:228
  15.6 2.6 %collective-permute-start.3 = (bf16[4,64,128]{2,1,0:T(8,128)(2,1)S(1)}, bf16[4,64,128]{2,1,0:T(8,128)(2,1)S(1)}, u32[]{:S(2)}, u32[]{:S(2)}) collective-permute-start(bf16[4,64,128]{2,1,0:T(8,128)(2,1)S(1)} %get-tuple-element.29), channel_id=1, source_target_pairs={{0,1},{2,3},{4,5},{6,7},{1,0},{3,2},{5,4},{7,6},{8,9},{10,11},{12,... | collective-permute-start | bytes 196616 | tf_op jit(solution)/shard_map/ppermute | solution.py:228
  18.2 0.0 copy-done
  18.2 0.6 shard_map.123
  18.8 0.0 collective-permute-done.2.y2_ref
  18.8 0.3 collective-permute-done.3.y1_ref
  19.1 0.0 collective-permute-done.x2_ref
  19.1 0.0 collective-permute-done.1.x1_ref
  19.1 0.0 copy-done.2
  19.1 0.0 copy-done.1
  19.1 2.0 %shard_map.124 = f32[8,40,128]{2,1,0:T(8,128)S(1)} custom-call(s32[96]{0:T(128)S(1)} %copy-done.1, s32[96]{0:T(128)S(1)} %copy-done.2, s32[1,96]{1,0:T(1,128)S(1)} %get-tuple-element.17.owner_ref, s32[1,96]{1,0:T(1,128)S(1)} %get-tuple-element.18.region_ref, bf16[96,64,128]{2,1,0:T(8,128)(2,1)S(1)} %get-tuple-element.21.k_ref, ...), custom_call_target="tpu_custom_call" | custom-call | tf_op jit(solution)/shard_map/pallas_call | solution.py:166
  21.1 10.1 %all_to_all.10.got_ref = f32[8,40,128]{2,1,0:T(8,128)S(1)} all-to-all(f32[8,40,128]{2,1,0:T(8,128)S(1)} %shard_map.124), channel_id=1, replica_groups=mesh['y'=8,'z'=12,'x'=4,'c'=2] {'x','c'}, dimensions={0} | all-to-all | bytes 327680 | tf_op jit(solution)/shard_map/all_to_all | solution.py:220
  31.2 0.7 %shard_map.125 = (f32[32,128]{1,0:T(8,128)}, f32[96,1,128]{2,1,0:T(1,128)S(1)}) custom-call(f32[8,40,128]{2,1,0:T(8,128)S(1)} %all_to_all.10.got_ref), custom_call_target="tpu_custom_call" | custom-call | tf_op jit(solution)/shard_map/pallas_call | solution.py:190
  31.9 31.8 %all_to_all.11.got_ref = f32[96,1,128]{2,1,0:T(1,128)S(1)} all-to-all(f32[96,1,128]{2,1,0:T(1,128)S(1)} %get-tuple-element.31), channel_id=1, replica_groups=mesh['y'=8,'z'=12,'x'=4,'c'=2] {'y','z'}, dimensions={0} | all-to-all | bytes 98304 | tf_op jit(solution)/shard_map/all_to_all | solution.py:220
  63.8 0.6 shard_map.126
Async XLA Ops:
  0.6 17.6 %copy-start = (bf16[96,4096]{1,0:T(8,128)(2,1)S(1)}, bf16[96,4096]{1,0:T(8,128)(2,1)}, u32[]{:S(2)}) copy-start(bf16[96,4096]{1,0:T(8,128)(2,1)} %tiles_ref.1) | copy-start | bytes 2359300
  0.6 18.5 %copy-start.2 = (s32[96]{0:T(128)S(1)}, s32[96]{0:T(128)}, u32[]{:S(2)}) copy-start(s32[96]{0:T(128)} %cols_ref.1) | copy-start | bytes 1156
  0.7 18.5 %copy-start.1 = (s32[96]{0:T(128)S(1)}, s32[96]{0:T(128)}, u32[]{:S(2)}) copy-start(s32[96]{0:T(128)} %rows_ref.1) | copy-start | bytes 1156
  2.5 16.6 %collective-permute-start = (bf16[12,64,128]{2,1,0:T(8,128)(2,1)S(1)}, bf16[12,64,128]{2,1,0:T(8,128)(2,1)S(1)}, u32[]{:S(2)}, u32[]{:S(2)}) collective-permute-start(bf16[12,64,128]{2,1,0:T(8,128)(2,1)S(1)} %get-tuple-element.26), channel_id=1, source_target_pairs={{8,16},{24,32},{40,48},{56,64},{72,80},{88,96},{104,112},{120,128}... | collective-permute-start | bytes 589832 | tf_op jit(solution)/shard_map/ppermute | solution.py:228
  3.2 15.9 %collective-permute-start.1 = (bf16[12,64,128]{2,1,0:T(8,128)(2,1)S(1)}, bf16[12,64,128]{2,1,0:T(8,128)(2,1)S(1)}, u32[]{:S(2)}, u32[]{:S(2)}) collective-permute-start(bf16[12,64,128]{2,1,0:T(8,128)(2,1)S(1)} %get-tuple-element.27), channel_id=1, source_target_pairs={{0,8},{16,24},{32,40},{48,56},{64,72},{80,88},{96,104},{112,120},{... | collective-permute-start | bytes 589832 | tf_op jit(solution)/shard_map/ppermute | solution.py:228
  11.4 7.5 %collective-permute-start.2 = (bf16[4,64,128]{2,1,0:T(8,128)(2,1)S(1)}, bf16[4,64,128]{2,1,0:T(8,128)(2,1)S(1)}, u32[]{:S(2)}, u32[]{:S(2)}) collective-permute-start(bf16[4,64,128]{2,1,0:T(8,128)(2,1)S(1)} %get-tuple-element.28), channel_id=1, source_target_pairs={{1,2},{3,4},{5,6},{2,1},{4,3},{6,5},{9,10},{11,12},{13,14},{10,9},... | collective-permute-start | bytes 196616 | tf_op jit(solution)/shard_map/ppermute | solution.py:228
  15.6 3.5 %collective-permute-start.3 = (bf16[4,64,128]{2,1,0:T(8,128)(2,1)S(1)}, bf16[4,64,128]{2,1,0:T(8,128)(2,1)S(1)}, u32[]{:S(2)}, u32[]{:S(2)}) collective-permute-start(bf16[4,64,128]{2,1,0:T(8,128)(2,1)S(1)} %get-tuple-element.29), channel_id=1, source_target_pairs={{0,1},{2,3},{4,5},{6,7},{1,0},{3,2},{5,4},{7,6},{8,9},{10,11},{12,... | collective-permute-start | bytes 196616 | tf_op jit(solution)/shard_map/ppermute | solution.py:228

commit v6 on v5

--- a/solution.py
+++ b/solution.py
@@ -158,8 +158,9 @@
             + jnp.dot(onehot, low, preferred_element_type=F32))
     place = lax.broadcasted_iota(jnp.int32, (8, LANES), 0)
     for o in range(OWNERS):
-        sent_ref[o, :NREG, :] = sums[o * NREG:(o + 1) * NREG, :]
-        sent_ref[o, NREG:, :] = jnp.where(place == 1, energy_total, totals_ref[o])
+        slot = o % 2 * (OWNERS // 2) + o // 2
+        sent_ref[slot, :NREG, :] = sums[o * NREG:(o + 1) * NREG, :]
+        sent_ref[slot, NREG:, :] = jnp.where(place == 1, energy_total, totals_ref[o])
 
 
 def elements(rows, cols, owner, region, k, factor, wide, totals, ul, x2, x1, y2, y1):
@@ -228,7 +229,7 @@
     halos = [lax.ppermute(face, axes, pairs) for face, (axes, pairs) in zip(faces, plans)]
     k, factor, wide, totals = stiffness(density, weight, owner, region, tiles)
     sent = elements(tile_rows, tile_cols, owner, region, k, factor, wide, totals, ul, *halos)
-    filtered, energy = regions(exchange(sent, ("x", "c")), ny * nz)
+    filtered, energy = regions(exchange(sent, ("c", "x")), ny * nz)
     compliance = last(exchange(energy, ("y", "z")), math.sqrt(NT * ny * nz * nx * nc))
     return (filtered, compliance)
 

time: 64.7 us -> 64.6 us (level)
  no operation moved by 1% of the time
where the time goes in v6:
time: 64.6 us; the launch traced here: 64.3 us
  blocking collectives  41.9 us (65%)
  starting transfers between devices  15.7 us (24%)
  Pallas kernels  5.72 us (9%)
  between operations  0.74 us (1%)
    all_to_all x2, blocking collectives, exchange(): return lax.all_to_all(x, axes, split_axis=0, concat_axis=0, tiled=True)  41.9 us
    ppermute x4, starting transfers between devices, shards(): lax.ppermute(face, axes, pairs)  15.7 us
    pallas_call x1, Pallas kernels, elements(): pl.pallas_call(element_kernel, out_shape=jax.ShapeDtypeStruct((OWNERS, SE...  1.98 us
    pallas_call x1, Pallas kernels, pack(): pl.pallas_call(pack_kernel, out_shape=[jax.ShapeDtypeStruct((n, BS, LANES...  1.84 us
  transfers between devices with their start and end apart: 4, of which 1 were waited for; matrix products, arithmetic and copies ran while one was open for 0% of the time, Pallas kernels for 1%

profile of v6, /device:TPU:1, one launch (start us, length us, event | category | flops | bytes accessed | tf_op | source)
XLA Modules:
  0.0 64.3 jit_solution(11287142405961618090)
XLA Ops:
  0.6 0.0 copy-start
  0.6 0.0 copy-start.2
  0.7 0.0 copy-start.1
  0.7 1.8 %shard_map.122 = (bf16[64,64,128]{2,1,0:T(8,128)(2,1)S(1)}, bf16[12,64,128]{2,1,0:T(8,128)(2,1)S(1)}, bf16[12,64,128]{2,1,0:T(8,128)(2,1)S(1)}, bf16[4,64,128]{2...) custom-call(s32[1,2,12]{2,1,0:T(2,128)} %fx_ref.1, ...), custom_call_target="tpu_custom_call" | custom-call | tf_op jit(solution)/shard_map/pallas_call | solution.py:61
  2.5 0.7 %collective-permute-start = (bf16[12,64,128]{2,1,0:T(8,128)(2,1)S(1)}, bf16[12,64,128]{2,1,0:T(8,128)(2,1)S(1)}, u32[]{:S(2)}, u32[]{:S(2)}) collective-permute-start(bf16[12,64,128]{2,1,0:T(8,128)(2,1)S(1)} %get-tuple-element.26), channel_id=1, source_target_pairs={{8,16},{24,32},{40,48},{56,64},{72,80},{88,96},{104,112},{120,128}... | collective-permute-start | bytes 589832 | tf_op jit(solution)/shard_map/ppermute | solution.py:229
  3.2 8.2 %collective-permute-start.1 = (bf16[12,64,128]{2,1,0:T(8,128)(2,1)S(1)}, bf16[12,64,128]{2,1,0:T(8,128)(2,1)S(1)}, u32[]{:S(2)}, u32[]{:S(2)}) collective-permute-start(bf16[12,64,128]{2,1,0:T(8,128)(2,1)S(1)} %get-tuple-element.27), channel_id=1, source_target_pairs={{0,8},{16,24},{32,40},{48,56},{64,72},{80,88},{96,104},{112,120},{... | collective-permute-start | bytes 589832 | tf_op jit(solution)/shard_map/ppermute | solution.py:229
  11.4 4.2 %collective-permute-start.2 = (bf16[4,64,128]{2,1,0:T(8,128)(2,1)S(1)}, bf16[4,64,128]{2,1,0:T(8,128)(2,1)S(1)}, u32[]{:S(2)}, u32[]{:S(2)}) collective-permute-start(bf16[4,64,128]{2,1,0:T(8,128)(2,1)S(1)} %get-tuple-element.28), channel_id=1, source_target_pairs={{1,2},{3,4},{5,6},{2,1},{4,3},{6,5},{9,10},{11,12},{13,14},{10,9},... | collective-permute-start | bytes 196616 | tf_op jit(solution)/shard_map/ppermute | solution.py:229
  15.6 2.6 %collective-permute-start.3 = (bf16[4,64,128]{2,1,0:T(8,128)(2,1)S(1)}, bf16[4,64,128]{2,1,0:T(8,128)(2,1)S(1)}, u32[]{:S(2)}, u32[]{:S(2)}) collective-permute-start(bf16[4,64,128]{2,1,0:T(8,128)(2,1)S(1)} %get-tuple-element.29), channel_id=1, source_target_pairs={{0,1},{2,3},{4,5},{6,7},{1,0},{3,2},{5,4},{7,6},{8,9},{10,11},{12,... | collective-permute-start | bytes 196616 | tf_op jit(solution)/shard_map/ppermute | solution.py:229
  18.2 0.0 copy-done
  18.2 0.6 shard_map.123
  18.8 0.0 collective-permute-done.2.y2_ref
  18.8 0.3 collective-permute-done.3.y1_ref
  19.1 0.0 collective-permute-done.x2_ref
  19.1 0.0 collective-permute-done.1.x1_ref
  19.1 0.0 copy-done.2
  19.1 0.0 copy-done.1
  19.1 2.0 %shard_map.124 = f32[8,40,128]{2,1,0:T(8,128)S(1)} custom-call(s32[96]{0:T(128)S(1)} %copy-done.1, s32[96]{0:T(128)S(1)} %copy-done.2, s32[1,96]{1,0:T(1,128)S(1)} %get-tuple-element.17.owner_ref, s32[1,96]{1,0:T(1,128)S(1)} %get-tuple-element.18.region_ref, bf16[96,64,128]{2,1,0:T(8,128)(2,1)S(1)} %get-tuple-element.21.k_ref, ...), custom_call_target="tpu_custom_call" | custom-call | tf_op jit(solution)/shard_map/pallas_call | solution.py:167
  21.1 10.0 %all_to_all.10.got_ref = f32[8,40,128]{2,1,0:T(8,128)S(1)} all-to-all(f32[8,40,128]{2,1,0:T(8,128)S(1)} %shard_map.124), channel_id=1, replica_groups=mesh['y'=8,'z'=12,'x'=4,'c'=2] {'c','x'}, dimensions={0} | all-to-all | bytes 327680 | tf_op jit(solution)/shard_map/all_to_all | solution.py:221
  31.2 0.7 %shard_map.125 = (f32[32,128]{1,0:T(8,128)}, f32[96,1,128]{2,1,0:T(1,128)S(1)}) custom-call(f32[8,40,128]{2,1,0:T(8,128)S(1)} %all_to_all.10.got_ref), custom_call_target="tpu_custom_call" | custom-call | tf_op jit(solution)/shard_map/pallas_call | solution.py:191
  31.9 31.8 %all_to_all.11.got_ref = f32[96,1,128]{2,1,0:T(1,128)S(1)} all-to-all(f32[96,1,128]{2,1,0:T(1,128)S(1)} %get-tuple-element.31), channel_id=1, replica_groups=mesh['y'=8,'z'=12,'x'=4,'c'=2] {'y','z'}, dimensions={0} | all-to-all | bytes 98304 | tf_op jit(solution)/shard_map/all_to_all | solution.py:221
  63.7 0.6 shard_map.126
Async XLA Ops:
  0.6 17.6 %copy-start = (bf16[96,4096]{1,0:T(8,128)(2,1)S(1)}, bf16[96,4096]{1,0:T(8,128)(2,1)}, u32[]{:S(2)}) copy-start(bf16[96,4096]{1,0:T(8,128)(2,1)} %tiles_ref.1) | copy-start | bytes 2359300
  0.6 18.5 %copy-start.2 = (s32[96]{0:T(128)S(1)}, s32[96]{0:T(128)}, u32[]{:S(2)}) copy-start(s32[96]{0:T(128)} %cols_ref.1) | copy-start | bytes 1156
  0.7 18.5 %copy-start.1 = (s32[96]{0:T(128)S(1)}, s32[96]{0:T(128)}, u32[]{:S(2)}) copy-start(s32[96]{0:T(128)} %rows_ref.1) | copy-start | bytes 1156
  2.5 16.6 %collective-permute-start = (bf16[12,64,128]{2,1,0:T(8,128)(2,1)S(1)}, bf16[12,64,128]{2,1,0:T(8,128)(2,1)S(1)}, u32[]{:S(2)}, u32[]{:S(2)}) collective-permute-start(bf16[12,64,128]{2,1,0:T(8,128)(2,1)S(1)} %get-tuple-element.26), channel_id=1, source_target_pairs={{8,16},{24,32},{40,48},{56,64},{72,80},{88,96},{104,112},{120,128}... | collective-permute-start | bytes 589832 | tf_op jit(solution)/shard_map/ppermute | solution.py:229
  3.2 15.9 %collective-permute-start.1 = (bf16[12,64,128]{2,1,0:T(8,128)(2,1)S(1)}, bf16[12,64,128]{2,1,0:T(8,128)(2,1)S(1)}, u32[]{:S(2)}, u32[]{:S(2)}) collective-permute-start(bf16[12,64,128]{2,1,0:T(8,128)(2,1)S(1)} %get-tuple-element.27), channel_id=1, source_target_pairs={{0,8},{16,24},{32,40},{48,56},{64,72},{80,88},{96,104},{112,120},{... | collective-permute-start | bytes 589832 | tf_op jit(solution)/shard_map/ppermute | solution.py:229
  11.4 7.5 %collective-permute-start.2 = (bf16[4,64,128]{2,1,0:T(8,128)(2,1)S(1)}, bf16[4,64,128]{2,1,0:T(8,128)(2,1)S(1)}, u32[]{:S(2)}, u32[]{:S(2)}) collective-permute-start(bf16[4,64,128]{2,1,0:T(8,128)(2,1)S(1)} %get-tuple-element.28), channel_id=1, source_target_pairs={{1,2},{3,4},{5,6},{2,1},{4,3},{6,5},{9,10},{11,12},{13,14},{10,9},... | collective-permute-start | bytes 196616 | tf_op jit(solution)/shard_map/ppermute | solution.py:229
  15.6 3.5 %collective-permute-start.3 = (bf16[4,64,128]{2,1,0:T(8,128)(2,1)S(1)}, bf16[4,64,128]{2,1,0:T(8,128)(2,1)S(1)}, u32[]{:S(2)}, u32[]{:S(2)}) collective-permute-start(bf16[4,64,128]{2,1,0:T(8,128)(2,1)S(1)} %get-tuple-element.29), channel_id=1, source_target_pairs={{0,1},{2,3},{4,5},{6,7},{1,0},{3,2},{5,4},{7,6},{8,9},{10,11},{12,... | collective-permute-start | bytes 196616 | tf_op jit(solution)/shard_map/ppermute | solution.py:229

commit v7 on v6

--- a/solution.py
+++ b/solution.py
@@ -19,7 +19,7 @@
 LANES = 128
 HALF = BS // 2
 SENT_ROWS = 40
-GROUP = 48
+GROUP = 96
 F32 = jnp.float32
 BF16 = jnp.bfloat16
 VMEM = pl.BlockSpec(memory_space=pltpu.VMEM)

time: 64.6 us -> 64.5 us (level)
  no operation moved by 1% of the time
where the time goes in v7:
time: 64.5 us; the launch traced here: 64.2 us
  blocking collectives  41.9 us (65%)
  starting transfers between devices  15.7 us (24%)
  Pallas kernels  5.62 us (9%)
  between operations  0.74 us (1%)
    all_to_all x2, blocking collectives, exchange(): return lax.all_to_all(x, axes, split_axis=0, concat_axis=0, tiled=True)  41.9 us
    ppermute x4, starting transfers between devices, shards(): lax.ppermute(face, axes, pairs)  15.7 us
    pallas_call x1, Pallas kernels, elements(): pl.pallas_call(element_kernel, out_shape=jax.ShapeDtypeStruct((OWNERS, SE...  1.89 us
    pallas_call x1, Pallas kernels, pack(): pl.pallas_call(pack_kernel, out_shape=[jax.ShapeDtypeStruct((n, BS, LANES...  1.84 us
  transfers between devices with their start and end apart: 4, of which 1 were waited for; matrix products, arithmetic and copies ran while one was open for 0% of the time, Pallas kernels for 1%

profile of v7, /device:TPU:1, one launch (start us, length us, event | category | flops | bytes accessed | tf_op | source)
XLA Modules:
  0.0 64.2 jit_solution(16277384023642751514)
XLA Ops:
  0.6 0.0 copy-start
  0.6 0.0 copy-start.2
  0.7 0.0 copy-start.1
  0.7 1.8 %shard_map.122 = (bf16[64,64,128]{2,1,0:T(8,128)(2,1)S(1)}, bf16[12,64,128]{2,1,0:T(8,128)(2,1)S(1)}, bf16[12,64,128]{2,1,0:T(8,128)(2,1)S(1)}, bf16[4,64,128]{2...) custom-call(s32[1,2,12]{2,1,0:T(2,128)} %fx_ref.1, ...), custom_call_target="tpu_custom_call" | custom-call | tf_op jit(solution)/shard_map/pallas_call | solution.py:61
  2.5 0.7 %collective-permute-start = (bf16[12,64,128]{2,1,0:T(8,128)(2,1)S(1)}, bf16[12,64,128]{2,1,0:T(8,128)(2,1)S(1)}, u32[]{:S(2)}, u32[]{:S(2)}) collective-permute-start(bf16[12,64,128]{2,1,0:T(8,128)(2,1)S(1)} %get-tuple-element.26), channel_id=1, source_target_pairs={{8,16},{24,32},{40,48},{56,64},{72,80},{88,96},{104,112},{120,128}... | collective-permute-start | bytes 589832 | tf_op jit(solution)/shard_map/ppermute | solution.py:229
  3.2 8.2 %collective-permute-start.1 = (bf16[12,64,128]{2,1,0:T(8,128)(2,1)S(1)}, bf16[12,64,128]{2,1,0:T(8,128)(2,1)S(1)}, u32[]{:S(2)}, u32[]{:S(2)}) collective-permute-start(bf16[12,64,128]{2,1,0:T(8,128)(2,1)S(1)} %get-tuple-element.27), channel_id=1, source_target_pairs={{0,8},{16,24},{32,40},{48,56},{64,72},{80,88},{96,104},{112,120},{... | collective-permute-start | bytes 589832 | tf_op jit(solution)/shard_map/ppermute | solution.py:229
  11.4 4.2 %collective-permute-start.2 = (bf16[4,64,128]{2,1,0:T(8,128)(2,1)S(1)}, bf16[4,64,128]{2,1,0:T(8,128)(2,1)S(1)}, u32[]{:S(2)}, u32[]{:S(2)}) collective-permute-start(bf16[4,64,128]{2,1,0:T(8,128)(2,1)S(1)} %get-tuple-element.28), channel_id=1, source_target_pairs={{1,2},{3,4},{5,6},{2,1},{4,3},{6,5},{9,10},{11,12},{13,14},{10,9},... | collective-permute-start | bytes 196616 | tf_op jit(solution)/shard_map/ppermute | solution.py:229
  15.6 2.6 %collective-permute-start.3 = (bf16[4,64,128]{2,1,0:T(8,128)(2,1)S(1)}, bf16[4,64,128]{2,1,0:T(8,128)(2,1)S(1)}, u32[]{:S(2)}, u32[]{:S(2)}) collective-permute-start(bf16[4,64,128]{2,1,0:T(8,128)(2,1)S(1)} %get-tuple-element.29), channel_id=1, source_target_pairs={{0,1},{2,3},{4,5},{6,7},{1,0},{3,2},{5,4},{7,6},{8,9},{10,11},{12,... | collective-permute-start | bytes 196616 | tf_op jit(solution)/shard_map/ppermute | solution.py:229
  18.2 0.0 copy-done
  18.2 0.6 shard_map.123
  18.8 0.0 collective-permute-done.2.y2_ref
  18.8 0.3 collective-permute-done.3.y1_ref
  19.1 0.0 collective-permute-done.x2_ref
  19.1 0.0 collective-permute-done.1.x1_ref
  19.1 0.0 copy-done.2
  19.1 0.0 copy-done.1
  19.1 1.9 %shard_map.124 = f32[8,40,128]{2,1,0:T(8,128)S(1)} custom-call(s32[96]{0:T(128)S(1)} %copy-done.1, s32[96]{0:T(128)S(1)} %copy-done.2, s32[1,96]{1,0:T(1,128)S(1)} %get-tuple-element.17.owner_ref, s32[1,96]{1,0:T(1,128)S(1)} %get-tuple-element.18.region_ref, bf16[96,64,128]{2,1,0:T(8,128)(2,1)S(1)} %get-tuple-element.21.k_ref, ...), custom_call_target="tpu_custom_call" | custom-call | tf_op jit(solution)/shard_map/pallas_call | solution.py:167
  21.0 10.0 %all_to_all.10.got_ref = f32[8,40,128]{2,1,0:T(8,128)S(1)} all-to-all(f32[8,40,128]{2,1,0:T(8,128)S(1)} %shard_map.124), channel_id=1, replica_groups=mesh['y'=8,'z'=12,'x'=4,'c'=2] {'c','x'}, dimensions={0} | all-to-all | bytes 327680 | tf_op jit(solution)/shard_map/all_to_all | solution.py:221
  31.1 0.7 %shard_map.125 = (f32[32,128]{1,0:T(8,128)}, f32[96,1,128]{2,1,0:T(1,128)S(1)}) custom-call(f32[8,40,128]{2,1,0:T(8,128)S(1)} %all_to_all.10.got_ref), custom_call_target="tpu_custom_call" | custom-call | tf_op jit(solution)/shard_map/pallas_call | solution.py:191
  31.8 31.8 %all_to_all.11.got_ref = f32[96,1,128]{2,1,0:T(1,128)S(1)} all-to-all(f32[96,1,128]{2,1,0:T(1,128)S(1)} %get-tuple-element.31), channel_id=1, replica_groups=mesh['y'=8,'z'=12,'x'=4,'c'=2] {'y','z'}, dimensions={0} | all-to-all | bytes 98304 | tf_op jit(solution)/shard_map/all_to_all | solution.py:221
  63.6 0.6 shard_map.126
Async XLA Ops:
  0.6 17.6 %copy-start = (bf16[96,4096]{1,0:T(8,128)(2,1)S(1)}, bf16[96,4096]{1,0:T(8,128)(2,1)}, u32[]{:S(2)}) copy-start(bf16[96,4096]{1,0:T(8,128)(2,1)} %tiles_ref.1) | copy-start | bytes 2359300
  0.6 18.5 %copy-start.2 = (s32[96]{0:T(128)S(1)}, s32[96]{0:T(128)}, u32[]{:S(2)}) copy-start(s32[96]{0:T(128)} %cols_ref.1) | copy-start | bytes 1156
  0.7 18.5 %copy-start.1 = (s32[96]{0:T(128)S(1)}, s32[96]{0:T(128)}, u32[]{:S(2)}) copy-start(s32[96]{0:T(128)} %rows_ref.1) | copy-start | bytes 1156
  2.5 16.6 %collective-permute-start = (bf16[12,64,128]{2,1,0:T(8,128)(2,1)S(1)}, bf16[12,64,128]{2,1,0:T(8,128)(2,1)S(1)}, u32[]{:S(2)}, u32[]{:S(2)}) collective-permute-start(bf16[12,64,128]{2,1,0:T(8,128)(2,1)S(1)} %get-tuple-element.26), channel_id=1, source_target_pairs={{8,16},{24,32},{40,48},{56,64},{72,80},{88,96},{104,112},{120,128}... | collective-permute-start | bytes 589832 | tf_op jit(solution)/shard_map/ppermute | solution.py:229
  3.2 15.9 %collective-permute-start.1 = (bf16[12,64,128]{2,1,0:T(8,128)(2,1)S(1)}, bf16[12,64,128]{2,1,0:T(8,128)(2,1)S(1)}, u32[]{:S(2)}, u32[]{:S(2)}) collective-permute-start(bf16[12,64,128]{2,1,0:T(8,128)(2,1)S(1)} %get-tuple-element.27), channel_id=1, source_target_pairs={{0,8},{16,24},{32,40},{48,56},{64,72},{80,88},{96,104},{112,120},{... | collective-permute-start | bytes 589832 | tf_op jit(solution)/shard_map/ppermute | solution.py:229
  11.4 7.5 %collective-permute-start.2 = (bf16[4,64,128]{2,1,0:T(8,128)(2,1)S(1)}, bf16[4,64,128]{2,1,0:T(8,128)(2,1)S(1)}, u32[]{:S(2)}, u32[]{:S(2)}) collective-permute-start(bf16[4,64,128]{2,1,0:T(8,128)(2,1)S(1)} %get-tuple-element.28), channel_id=1, source_target_pairs={{1,2},{3,4},{5,6},{2,1},{4,3},{6,5},{9,10},{11,12},{13,14},{10,9},... | collective-permute-start | bytes 196616 | tf_op jit(solution)/shard_map/ppermute | solution.py:229
  15.6 3.5 %collective-permute-start.3 = (bf16[4,64,128]{2,1,0:T(8,128)(2,1)S(1)}, bf16[4,64,128]{2,1,0:T(8,128)(2,1)S(1)}, u32[]{:S(2)}, u32[]{:S(2)}) collective-permute-start(bf16[4,64,128]{2,1,0:T(8,128)(2,1)S(1)} %get-tuple-element.29), channel_id=1, source_target_pairs={{0,1},{2,3},{4,5},{6,7},{1,0},{3,2},{5,4},{7,6},{8,9},{10,11},{12,... | collective-permute-start | bytes 196616 | tf_op jit(solution)/shard_map/ppermute | solution.py:229
